TPU v7x, 32 devices: a whole 2x2x4 slice. The times are simulated.
32 devices in a mesh: dp: 4 (over y, core), seq: 8 (over z, x).
Axes of the slice: x: 2, y: 2, z: 4, core: 2. Of those that a mesh axis runs over, the one named last changes fastest.
Arguments:
- tokens: bfloat16 [8, 1024, 768], P('dp', 'seq'), may hold values from -8 to 8
- segments: int32 [8, 1024], P('dp'), may hold values from 0 to 3, as said below
- cotangent: bfloat16 [8, 1024, 768], P('dp', 'seq'), may hold values from -6 to 6
- w_qkv: bfloat16 [768, 2304], P(('dp', 'seq')), may hold values from -0.21875 to 0.21875
- bias_q: bfloat16 [768], P(('dp', 'seq')), may hold values from -3 to 3
- bias_v: bfloat16 [768], P(('dp', 'seq')), may hold values from -0.3125 to 0.3125
- w_out: bfloat16 [768, 768], P(('dp', 'seq')), may hold values from -3 to 3
- bias_out: bfloat16 [768], P(('dp', 'seq')), may hold values from -3 to 3
- gain_one: bfloat16 [768], P(('dp', 'seq')), may hold values from 0.099609375 to 1.8984375
- shift_one: bfloat16 [768], P(('dp', 'seq')), may hold values from -1.75 to 1.75
- w_up: bfloat16 [768, 3072], P(('dp', 'seq')), may hold values from -0.21875 to 0.21875
- bias_up: bfloat16 [3072], P(('dp', 'seq')), may hold values from -3 to 3
- w_down: bfloat16 [3072, 768], P(('dp', 'seq')), may hold values from -0.109375 to 0.109375
- bias_down: bfloat16 [768], P(('dp', 'seq')), may hold values from -3 to 3
- gain_two: bfloat16 [768], P(('dp', 'seq')), may hold values from 0.099609375 to 1.8984375
- shift_two: bfloat16 [768], P(('dp', 'seq')), may hold values from -1.75 to 1.75
Outputs:
- layer_out: bfloat16 [8, 1024, 768], P('dp', 'seq')
- grad_tokens: float32 [8, 1024, 768], P('dp', 'seq')
- grad_w_qkv: float32 [768, 2304], P(('dp', 'seq'))
- grad_bias_q: float32 [768], P(('dp', 'seq'))
- grad_bias_v: float32 [768], P(('dp', 'seq'))
- grad_w_out: float32 [768, 768], P(('dp', 'seq'))
- grad_bias_out: float32 [768], P(('dp', 'seq'))
- grad_gain_one: float32 [768], P(('dp', 'seq'))
- grad_shift_one: float32 [768], P(('dp', 'seq'))
- grad_w_up: float32 [768, 3072], P(('dp', 'seq'))
- grad_bias_up: float32 [3072], P(('dp', 'seq'))
- grad_w_down: float32 [3072, 768], P(('dp', 'seq'))
- grad_bias_down: float32 [768], P(('dp', 'seq'))
- grad_gain_two: float32 [768], P(('dp', 'seq'))
- grad_shift_two: float32 [768], P(('dp', 'seq'))
Inputs may be any that keep to these rules, and one draw needn't show every extreme that they name: `segments`: along each sequence the numbers start at 0 and never fall; a token attends to the tokens of its own sequence with its own number. In one sequence, drawn from the seed, of the 2 of each index of dp all numbers are 0.
All inputs are finite; a program needn't handle non-finite values.
Results may differ from a plain program's by a relative error of at most 0.015.
Values may be sent and summed in bfloat16 or wider, within the bound.
A program may use at most 192 MiB of HBM per device.

v0:
```python
import jax
import jax.numpy as jnp
from jax import lax
from jax.sharding import PartitionSpec as P

HEAD = 64
HEAD_GROUP = 4


masked_out = -1000000000.0
epsilon = 1e-05


def normalize(values, gain_row, offset):
    center = values - jnp.mean(values, axis=-1, keepdims=True)
    spread = jnp.mean(center * center, axis=-1, keepdims=True)
    return center * lax.rsqrt(spread + epsilon) * gain_row + offset


def exact_gelu(values):
    return jax.nn.gelu(values, approximate=False)


def contract_rows(first_op, second_op):
    return lax.dot_general(
        first_op, second_op, (((0,), (0,)), ((), ())), preferred_element_type=jnp.float32
    )


def contract_cols(first_op, second_op):
    return lax.dot_general(
        first_op, second_op, (((1,), (1,)), ((), ())), preferred_element_type=jnp.float32
    )


def column_sum(values):
    return jnp.sum(values.astype(jnp.float32), axis=0)


def group_scores(query_heads, key_heads, same_doc):
    scaled = jnp.einsum(
        "qhe,khe->hqk", query_heads, key_heads, preferred_element_type=jnp.float32
    ) * HEAD ** (-0.5)
    return jnp.where(same_doc[None], scaled, masked_out)


def head_slice(values, column, width):
    return lax.dynamic_slice_in_dim(values, column, width, 1).reshape(
        values.shape[0], HEAD_GROUP, HEAD
    )


def attend_forward(seq_item):
    queries, keys_all, values_all, same_doc = seq_item
    row_count = queries.shape[0]
    width = HEAD_GROUP * HEAD
    groups = queries.shape[1] // width

    def one_group(group_idx, state_tuple):
        outputs, log_sums = state_tuple
        column = group_idx * width
        scores = group_scores(
            head_slice(queries, column, width), head_slice(keys_all, column, width), same_doc
        )
        highest = jnp.max(scores, axis=2, keepdims=True)
        exponent = jnp.exp(scores - highest)
        denominator = jnp.sum(exponent, axis=2, keepdims=True)
        weights = (exponent / denominator).astype(jnp.bfloat16)
        combined = jnp.einsum(
            "hqk,khe->qhe",
            weights,
            head_slice(values_all, column, width),
            preferred_element_type=jnp.float32,
        )
        outputs = lax.dynamic_update_slice_in_dim(
            outputs, combined.reshape(row_count, width), column, 1
        )
        log_part = (highest + jnp.log(denominator))[:, :, 0]
        log_sums = lax.dynamic_update_slice_in_dim(log_sums, log_part, group_idx * HEAD_GROUP, 0)
        return (outputs, log_sums)

    start_state = (
        jnp.zeros((row_count, queries.shape[1]), jnp.float32),
        jnp.zeros((queries.shape[1] // HEAD, row_count), jnp.float32),
    )
    return lax.fori_loop(0, groups, one_group, start_state)


def attend_query_side(seq_item):
    queries, keys_all, values_all, same_doc, log_sums, grad_mixed = seq_item
    row_count = queries.shape[0]
    width = HEAD_GROUP * HEAD
    groups = queries.shape[1] // width
    scale_factor = HEAD ** (-0.5)

    def one_group(group_idx, state_tuple):
        grad_query, deltas = state_tuple
        column = group_idx * width
        key_heads = head_slice(keys_all, column, width)
        log_part = lax.dynamic_slice_in_dim(log_sums, group_idx * HEAD_GROUP, HEAD_GROUP, 0)
        scores = group_scores(head_slice(queries, column, width), key_heads, same_doc)
        probs = jnp.exp(scores - log_part[:, :, None])
        grad_probs = jnp.einsum(
            "qhe,khe->hqk",
            head_slice(grad_mixed, column, width),
            head_slice(values_all, column, width),
            preferred_element_type=jnp.float32,
        )
        row_delta = jnp.sum(probs * grad_probs, axis=2, keepdims=True)
        grad_scores = (probs * (grad_probs - row_delta)).astype(jnp.bfloat16)
        query_term = (
            jnp.einsum("hqk,khe->qhe", grad_scores, key_heads, preferred_element_type=jnp.float32)
            * scale_factor
        )
        grad_query = lax.dynamic_update_slice_in_dim(
            grad_query, query_term.reshape(row_count, width), column, 1
        )
        deltas = lax.dynamic_update_slice_in_dim(
            deltas, row_delta[:, :, 0], group_idx * HEAD_GROUP, 0
        )
        return (grad_query, deltas)

    start_state = (
        jnp.zeros((row_count, queries.shape[1]), jnp.float32),
        jnp.zeros((queries.shape[1] // HEAD, row_count), jnp.float32),
    )
    return lax.fori_loop(0, groups, one_group, start_state)


def attend_key_side(seq_item):
    keys_own, values_own, queries_all, grad_all, log_all, delta_all, doc_mask = seq_item
    key_count = keys_own.shape[0]
    width = HEAD_GROUP * HEAD
    groups = keys_own.shape[1] // width
    scale_factor = HEAD ** (-0.5)

    def one_group(group_idx, state_tuple):
        grad_keys, grad_values = state_tuple
        column = group_idx * width
        query_heads = head_slice(queries_all, column, width)
        grad_heads = head_slice(grad_all, column, width)
        log_part = lax.dynamic_slice_in_dim(log_all, group_idx * HEAD_GROUP, HEAD_GROUP, 0)
        delta_part = lax.dynamic_slice_in_dim(delta_all, group_idx * HEAD_GROUP, HEAD_GROUP, 0)
        scores = group_scores(query_heads, head_slice(keys_own, column, width), doc_mask)
        probs = jnp.exp(scores - log_part[:, :, None])
        probs_low = probs.astype(jnp.bfloat16)
        grad_probs = jnp.einsum(
            "qhe,khe->hqk",
            grad_heads,
            head_slice(values_own, column, width),
            preferred_element_type=jnp.float32,
        )
        grad_scores = (probs * (grad_probs - delta_part[:, :, None])).astype(jnp.bfloat16)
        key_term = (
            jnp.einsum("hqk,qhe->khe", grad_scores, query_heads, preferred_element_type=jnp.float32)
            * scale_factor
        )
        value_term = jnp.einsum(
            "hqk,qhe->khe", probs_low, grad_heads, preferred_element_type=jnp.float32
        )
        grad_keys = lax.dynamic_update_slice_in_dim(
            grad_keys, key_term.reshape(key_count, width), column, 1
        )
        grad_values = lax.dynamic_update_slice_in_dim(
            grad_values, value_term.reshape(key_count, width), column, 1
        )
        return (grad_keys, grad_values)

    model_width = keys_own.shape[1]
    start_state = (
        jnp.zeros((key_count, model_width), jnp.float32),
        jnp.zeros((key_count, model_width), jnp.float32),
    )
    return lax.fori_loop(0, groups, one_group, start_state)


def on_device(
    tokens,
    segments,
    cotangent,
    w_qkv,
    bias_q,
    bias_v,
    w_out,
    bias_out,
    gain_one,
    shift_one,
    w_up,
    bias_up,
    w_down,
    bias_down,
    gain_two,
    shift_two,
):
    gathered = (
        lax.all_gather(w_qkv, ("dp", "seq"), axis=0, tiled=True),
        lax.all_gather(bias_q, ("dp", "seq"), axis=0, tiled=True),
        lax.all_gather(bias_v, ("dp", "seq"), axis=0, tiled=True),
        lax.all_gather(w_out, ("dp", "seq"), axis=0, tiled=True),
        lax.all_gather(bias_out, ("dp", "seq"), axis=0, tiled=True),
        lax.all_gather(gain_one, ("dp", "seq"), axis=0, tiled=True),
        lax.all_gather(shift_one, ("dp", "seq"), axis=0, tiled=True),
        lax.all_gather(w_up, ("dp", "seq"), axis=0, tiled=True),
        lax.all_gather(bias_up, ("dp", "seq"), axis=0, tiled=True),
        lax.all_gather(w_down, ("dp", "seq"), axis=0, tiled=True),
        lax.all_gather(bias_down, ("dp", "seq"), axis=0, tiled=True),
        lax.all_gather(gain_two, ("dp", "seq"), axis=0, tiled=True),
        lax.all_gather(shift_two, ("dp", "seq"), axis=0, tiled=True),
    )
    seq_count, slice_len, model_width = tokens.shape
    row_total = seq_count * slice_len
    inputs = tokens.reshape(row_total, model_width)
    qkv_bias = jnp.concatenate(
        [
            gathered[1].astype(jnp.float32),
            jnp.zeros((model_width,), jnp.float32),
            gathered[2].astype(jnp.float32),
        ]
    )
    projected = (
        jnp.dot(inputs, gathered[0], preferred_element_type=jnp.float32) + qkv_bias
    ).astype(jnp.bfloat16)
    query_low = projected[:, :model_width].reshape(seq_count, slice_len, model_width)
    key_low = projected[:, model_width : 2 * model_width].reshape(seq_count, slice_len, model_width)
    value_low = projected[:, 2 * model_width :].reshape(seq_count, slice_len, model_width)
    keys_all, values_all = (
        lax.all_gather(key_low, "seq", axis=1, tiled=True),
        lax.all_gather(value_low, "seq", axis=1, tiled=True),
    )
    first_row = lax.axis_index("seq") * slice_len
    own_docs = lax.dynamic_slice_in_dim(segments, first_row, slice_len, 1)
    same_doc = own_docs[:, :, None] == segments[:, None, :]
    mixed, log_sums = lax.map(attend_forward, (query_low, keys_all, values_all, same_doc))
    mixed_low = mixed.reshape(row_total, model_width).astype(jnp.bfloat16)
    branch = jnp.dot(mixed_low, gathered[3], preferred_element_type=jnp.float32) + gathered[
        4
    ].astype(jnp.float32)
    normed_one, norm_one_back = jax.vjp(
        normalize,
        inputs.astype(jnp.float32) + branch,
        gathered[5].astype(jnp.float32),
        gathered[6].astype(jnp.float32),
    )
    normed_low = normed_one.astype(jnp.bfloat16)
    hidden = jnp.dot(normed_low, gathered[7], preferred_element_type=jnp.float32) + gathered[
        8
    ].astype(jnp.float32)
    activated, gelu_back = jax.vjp(exact_gelu, hidden)
    activated_low = activated.astype(jnp.bfloat16)
    feed = jnp.dot(activated_low, gathered[9], preferred_element_type=jnp.float32) + gathered[
        10
    ].astype(jnp.float32)
    result, norm_two_back = jax.vjp(
        normalize,
        normed_one + feed,
        gathered[11].astype(jnp.float32),
        gathered[12].astype(jnp.float32),
    )
    weights_back = (
        lax.all_gather(w_qkv, ("dp", "seq"), axis=0, tiled=True),
        lax.all_gather(bias_q, ("dp", "seq"), axis=0, tiled=True),
        lax.all_gather(bias_v, ("dp", "seq"), axis=0, tiled=True),
        lax.all_gather(w_out, ("dp", "seq"), axis=0, tiled=True),
        lax.all_gather(bias_out, ("dp", "seq"), axis=0, tiled=True),
        lax.all_gather(gain_one, ("dp", "seq"), axis=0, tiled=True),
        lax.all_gather(shift_one, ("dp", "seq"), axis=0, tiled=True),
        lax.all_gather(w_up, ("dp", "seq"), axis=0, tiled=True),
        lax.all_gather(bias_up, ("dp", "seq"), axis=0, tiled=True),
        lax.all_gather(w_down, ("dp", "seq"), axis=0, tiled=True),
        lax.all_gather(bias_down, ("dp", "seq"), axis=0, tiled=True),
        lax.all_gather(gain_two, ("dp", "seq"), axis=0, tiled=True),
        lax.all_gather(shift_two, ("dp", "seq"), axis=0, tiled=True),
    )
    grad_sum_two, grad_gain_two, grad_shift_two = norm_two_back(
        cotangent.reshape(row_total, model_width).astype(jnp.float32)
    )
    grad_feed = grad_sum_two.astype(jnp.bfloat16)
    grad_w_down = contract_rows(activated_low, grad_feed)
    grad_bias_down = column_sum(grad_feed)
    (grad_hidden,) = gelu_back(contract_cols(grad_feed, weights_back[9]))
    grad_hidden_low = grad_hidden.astype(jnp.bfloat16)
    grad_w_up = contract_rows(normed_low, grad_hidden_low)
    grad_bias_up = column_sum(grad_hidden_low)
    grad_normed = grad_sum_two + contract_cols(grad_hidden_low, weights_back[7])
    grad_sum_one, grad_gain_one, grad_shift_one = norm_one_back(grad_normed)
    grad_branch = grad_sum_one.astype(jnp.bfloat16)
    grad_w_out = contract_rows(mixed_low, grad_branch)
    grad_bias_out = column_sum(grad_branch)
    grad_mixed = (
        contract_cols(grad_branch, weights_back[3])
        .astype(jnp.bfloat16)
        .reshape(seq_count, slice_len, model_width)
    )
    keys_back, values_back = (
        lax.all_gather(key_low, "seq", axis=1, tiled=True),
        lax.all_gather(value_low, "seq", axis=1, tiled=True),
    )
    grad_query, row_deltas = lax.map(
        attend_query_side, (query_low, keys_back, values_back, same_doc, log_sums, grad_mixed)
    )
    queries_all, grad_mixed_all = (
        lax.all_gather(query_low, "seq", axis=1, tiled=True),
        lax.all_gather(grad_mixed, "seq", axis=1, tiled=True),
    )
    log_all, delta_all = (
        lax.all_gather(log_sums, "seq", axis=2, tiled=True),
        lax.all_gather(row_deltas, "seq", axis=2, tiled=True),
    )
    doc_mask = segments[:, :, None] == own_docs[:, None, :]
    grad_key_own, grad_value_own = lax.map(
        attend_key_side,
        (key_low, value_low, queries_all, grad_mixed_all, log_all, delta_all, doc_mask),
    )
    grad_proj = jnp.concatenate(
        [
            grad_query.astype(jnp.bfloat16),
            grad_key_own.astype(jnp.bfloat16),
            grad_value_own.astype(jnp.bfloat16),
        ],
        axis=2,
    ).reshape(row_total, 3 * model_width)
    grad_w_qkv = contract_rows(inputs, grad_proj)
    grad_bias_q = column_sum(grad_proj[:, :model_width])
    grad_bias_v = column_sum(grad_proj[:, 2 * model_width :])
    grad_inputs = grad_sum_one + contract_cols(grad_proj, weights_back[0])
    owned = (
        lax.psum_scatter(grad_w_qkv, ("dp", "seq"), scatter_dimension=0, tiled=True),
        lax.psum_scatter(grad_bias_q, ("dp", "seq"), scatter_dimension=0, tiled=True),
        lax.psum_scatter(grad_bias_v, ("dp", "seq"), scatter_dimension=0, tiled=True),
        lax.psum_scatter(grad_w_out, ("dp", "seq"), scatter_dimension=0, tiled=True),
        lax.psum_scatter(grad_bias_out, ("dp", "seq"), scatter_dimension=0, tiled=True),
        lax.psum_scatter(grad_gain_one, ("dp", "seq"), scatter_dimension=0, tiled=True),
        lax.psum_scatter(grad_shift_one, ("dp", "seq"), scatter_dimension=0, tiled=True),
        lax.psum_scatter(grad_w_up, ("dp", "seq"), scatter_dimension=0, tiled=True),
        lax.psum_scatter(grad_bias_up, ("dp", "seq"), scatter_dimension=0, tiled=True),
        lax.psum_scatter(grad_w_down, ("dp", "seq"), scatter_dimension=0, tiled=True),
        lax.psum_scatter(grad_bias_down, ("dp", "seq"), scatter_dimension=0, tiled=True),
        lax.psum_scatter(grad_gain_two, ("dp", "seq"), scatter_dimension=0, tiled=True),
        lax.psum_scatter(grad_shift_two, ("dp", "seq"), scatter_dimension=0, tiled=True),
    )
    final_out = result.astype(jnp.bfloat16).reshape(seq_count, slice_len, model_width)
    grad_tokens = grad_inputs.reshape(seq_count, slice_len, model_width)
    return (final_out, grad_tokens) + tuple(owned)


def solution(mesh):
    return jax.shard_map(
        on_device,
        mesh=mesh,
        in_specs=(
            P("dp", "seq", None),
            P("dp", None),
            P("dp", "seq", None),
            P(("dp", "seq"), None),
            P(("dp", "seq")),
            P(("dp", "seq")),
            P(("dp", "seq"), None),
            P(("dp", "seq")),
            P(("dp", "seq")),
            P(("dp", "seq")),
            P(("dp", "seq"), None),
            P(("dp", "seq")),
            P(("dp", "seq"), None),
            P(("dp", "seq")),
            P(("dp", "seq")),
            P(("dp", "seq")),
        ),
        out_specs=(
            P("dp", "seq", None),
            P("dp", "seq", None),
            P(("dp", "seq"), None),
            P(("dp", "seq")),
            P(("dp", "seq")),
            P(("dp", "seq"), None),
            P(("dp", "seq")),
            P(("dp", "seq")),
            P(("dp", "seq")),
            P(("dp", "seq"), None),
            P(("dp", "seq")),
            P(("dp", "seq"), None),
            P(("dp", "seq")),
            P(("dp", "seq")),
            P(("dp", "seq")),
        ),
        check_vma=False,
    )
```

profile of v0, /device:TPU:0, one launch (start us, length us, event | category | flops | bytes accessed | tf_op | source)
XLA Modules:
  0.0 1038.8 jit_solution(3616839903468497557)
XLA Ops:
  15.5 42.6 %all-reduce.19 = (bf16[3072]{0:T(1024)(128)(2,1)S(1)}, bf16[768]{0:T(1024)(128)(2,1)S(1)}, bf16[768]{0:T(1024)(128)(2,1)S(1)}, bf16[768]{0:T(1024)(128)(2,1)S(1)...) all-reduce(bf16[3072]{0:T(1024)(128)(2,1)S(1)} %dynamic-update-slic, ...), channel_id=1, replica_groups=mesh['dp'=4,'seq'=8] {'dp','seq'}, use_global_device_ids=true, to_apply=%add.5 | all-reduce | flops 9216 | bytes 36864
  58.1 15.9 %all-gather.9.cloned.1.call-done = bf16[768,2304]{1,0:T(8,128)(2,1)} async-done(((bf16[24,2304]{1,0:T(8,128)(2,1)}), bf16[768,2304]{1,0:T(8,128)(2,1)}) %all-gather.9.cloned.1.call-update) | async-done | bytes 3538960 | tf_op jit(solution)/shard_map/all_gather | solution.py:196
  74.0 3.2 fusion.11
  87.4 52.9 %all-gather.11.cloned.1.call-done = bf16[2,1024,768]{1,2,0:T(8,128)(2,1)} async-done(((bf16[2,128,768]{1,2,0:T(8,128)(2,1)}), bf16[2,1024,768]{1,2,0:T(8,128)(2,1)}) %all-gather.11.cloned.1.call-update) | async-done | bytes 3145744 | tf_op jit(solution)/shard_map/all_gather | solution.py:227
  140.3 63.3 %all-gather.13.cloned.1.call-done = bf16[2,1024,768]{1,2,0:T(8,128)(2,1)} async-done(((bf16[2,128,768]{1,2,0:T(8,128)(2,1)}), bf16[2,1024,768]{1,2,0:T(8,128)(2,1)}) %all-gather.13.cloned.1.call-update) | async-done | bytes 3145744 | tf_op jit(solution)/shard_map/all_gather | solution.py:228
  204.2 34.2 %while.82 = (s32[]{:T(128)}, bf16[2,128,768]{2,1,0:T(8,128)(2,1)}, f32[2,12,128]{2,1,0:T(8,128)}, bf16[2,128,768]{1,2,0:T(8,128)(2,1)}, bf16[2,1024,768]{1,2,0:T...) while((s32[]{:T(128)}, bf16[2,128,768]{2,1,0:T(8,128)(2,1)}, ...), condition=%wide.region_5.6_spmd, body=%wide.region_0.5_spmd.sunk | while | flops 140508672 | bytes 18191872 | solution.py:233
  204.2 3.9 dynamic-slice_bitcast_fusion.28
  210.0 9.9 while.87
  221.4 3.9 dynamic-slice_bitcast_fusion.28
  227.1 9.9 while.87
  238.5 20.4 %all-gather.15.cloned.1.call-done = bf16[768,768]{1,0:T(8,128)(2,1)} async-done(((bf16[24,768]{1,0:T(8,128)(2,1)}), bf16[768,768]{1,0:T(8,128)(2,1)}) %all-gather.15.cloned.1.call-update) | async-done | bytes 1179664 | tf_op jit(solution)/shard_map/all_gather | solution.py:199
  258.8 1.9 fusion.34
  261.0 63.3 %all-gather.17.cloned.1.call-done = bf16[768,3072]{1,0:T(8,128)(2,1)} async-done(((bf16[24,3072]{1,0:T(8,128)(2,1)}), bf16[768,3072]{1,0:T(8,128)(2,1)}) %all-gather.17.cloned.1.call-update) | async-done | bytes 4718608 | tf_op jit(solution)/shard_map/all_gather | solution.py:203
  324.3 11.3 %multiply_convert_fusion.3 = (bf16[256,3072]{1,0:T(8,128)(2,1)S(1)}, f32[256,3072]{1,0:T(8,128)}, f32[256,3072]{1,0:T(8,128)}) fusion(f32[3072]{0:T(1024)S(1)} %copy-done.23, bf16[768,3072]{1,0:T(8,128)(2,1)} %all-gather.17.cloned.1.call-done, f32[256,768]{1,0:T(8,128)S(1)} %get-tuple-element.903, f32[768]{0:T(1024)S(1)} %copy-done.13, ...), kind=kOutput, calls=%fused_computation.71 | convolution fusion | flops 1260847104 | bytes 13389824 | tf_op jit(solution)/shard_map/dot_general | solution.py:245
  335.7 54.0 %all-gather.19.cloned.1.call-done = bf16[3072,768]{1,0:T(8,128)(2,1)} async-done(((bf16[96,768]{1,0:T(8,128)(2,1)}), bf16[3072,768]{1,0:T(8,128)(2,1)}) %all-gather.19.cloned.1.call-update) | async-done | bytes 4718608 | tf_op jit(solution)/shard_map/all_gather | solution.py:205
  389.7 4.0 fusion.35
  396.9 2.7 convert_reduce_fusion
  399.6 2.3 multiply_reduce_fusion.1
  404.4 1.9 copy.58
  406.4 1.9 fusion.37
  408.4 6.7 fusion.27
  416.8 33.3 %all_gather.80 = f32[2,12,1024]{2,1,0:T(8,128)} all-gather(f32[2,12,128]{2,1,0:T(8,128)S(1)} %copy-done.11), channel_id=1, replica_groups=mesh['dp'=4,'seq'=8] {'seq'}, dimensions={2}, use_global_device_ids=true | all-gather | bytes 110592 | tf_op jit(solution)/shard_map/all_gather | solution.py:306
  450.1 5.1 fusion.38
  455.9 34.1 %while.84 = (s32[]{:T(128)}, bf16[2,128,768]{1,2,0:T(8,128)(2,1)}, f32[2,12,128]{2,1,0:T(8,128)S(1)}, bf16[2,1024,768]{1,2,0:T(8,128)(2,1)}, f32[2,12,128]{2,1,0...) while((s32[]{:T(128)}, bf16[2,128,768]{1,2,0:T(8,128)(2,1)}, ...), condition=%wide.region_18.19_spmd, body=%wide.region_14.18_spmd.sunk | while | flops 205585920 | bytes 22856764 | solution.py:298
  455.9 3.8 dynamic-slice_bitcast_fusion.31
  461.8 10.5 %while.88 = (s32[]{:T(128)}, bf16[128,768]{0,1:T(8,128)(2,1)S(1)}, f32[12,128]{1,0:T(8,128)S(1)}, bf16[1024,768]{0,1:T(8,128)(2,1)}, pred[128,1024]{1,0:T(8,128)...) while((s32[]{:T(128)}, bf16[128,768]{0,1:T(8,128)(2,1)S(1)}, ...), condition=%wide.region_17.17_spmd, body=%wide.region_15.16_spmd.sunk | while | flops 205585920 | bytes 14891261 | solution.py:127
  473.0 3.8 dynamic-slice_bitcast_fusion.31
  478.9 10.5 %while.88 = (s32[]{:T(128)}, bf16[128,768]{0,1:T(8,128)(2,1)S(1)}, f32[12,128]{1,0:T(8,128)S(1)}, bf16[1024,768]{0,1:T(8,128)(2,1)}, pred[128,1024]{1,0:T(8,128)...) while((s32[]{:T(128)}, bf16[128,768]{0,1:T(8,128)(2,1)S(1)}, ...), condition=%wide.region_17.17_spmd, body=%wide.region_15.16_spmd.sunk | while | flops 205585920 | bytes 14891261 | solution.py:127
  490.1 32.9 %all_gather.81 = f32[2,12,1024]{2,1,0:T(8,128)} all-gather(f32[2,12,128]{2,1,0:T(8,128)S(1)} %get-tuple-element.607), channel_id=1, replica_groups=mesh['dp'=4,'seq'=8] {'seq'}, dimensions={2}, use_global_device_ids=true | all-gather | bytes 110592 | tf_op jit(solution)/shard_map/all_gather | solution.py:307
  524.6 77.4 %while.86 = (s32[]{:T(128)}, bf16[2,128,768]{1,2,0:T(8,128)(2,1)}, bf16[2,128,768]{1,2,0:T(8,128)(2,1)}, bf16[2,1024,768]{1,2,0:T(8,128)(2,1)}, bf16[2,1024,768]...) while((s32[]{:T(128)}, bf16[2,128,768]{1,2,0:T(8,128)(2,1)}, ...), condition=%wide.region_22.23_spmd, body=%wide.region_19.22_spmd.sunk | while | flops 272171008 | bytes 20219476 | solution.py:310
  524.6 3.9 dynamic-slice_bitcast_fusion.35
  534.7 25.4 %while.89 = (s32[]{:T(128)}, bf16[128,768]{0,1:T(8,128)(2,1)}, bf16[128,768]{0,1:T(8,128)(2,1)}, bf16[1024,768]{0,1:T(8,128)(2,1)}, pred[1024,128]{1,0:T(8,128)(...) while((s32[]{:T(128)}, bf16[128,768]{0,1:T(8,128)(2,1)}, ...), condition=%wide.region_21.21_spmd, body=%wide.region_20.20_spmd.sunk | while | flops 272171008 | bytes 11501837 | solution.py:174
  537.4 2.5 subtract_exponential_fusion.4
  545.9 2.5 subtract_exponential_fusion.4
  554.3 2.5 subtract_exponential_fusion.4
  563.3 3.9 dynamic-slice_bitcast_fusion.35
  567.2 1.7 dynamic-slice_bitcast_fusion.37
  573.4 25.3 %while.89 = (s32[]{:T(128)}, bf16[128,768]{0,1:T(8,128)(2,1)}, bf16[128,768]{0,1:T(8,128)(2,1)}, bf16[1024,768]{0,1:T(8,128)(2,1)}, pred[1024,128]{1,0:T(8,128)(...) while((s32[]{:T(128)}, bf16[128,768]{0,1:T(8,128)(2,1)}, ...), condition=%wide.region_21.21_spmd, body=%wide.region_20.20_spmd.sunk | while | flops 272171008 | bytes 11501837 | solution.py:174
  576.1 2.5 subtract_exponential_fusion.4
  584.6 2.5 subtract_exponential_fusion.4
  593.0 2.5 subtract_exponential_fusion.4
  602.0 5.3 convolution_bitcast_fusion
  607.3 8.0 copy.65
  617.6 39.7 %all-reduce.18 = (f32[768]{0:T(1024)S(1)}, f32[768]{0:T(1024)S(1)}, f32[768]{0:T(1024)S(1)}, f32[768]{0:T(1024)S(1)}, f32[768]{0:T(1024)S(1)}, /*index=5*/f32[30...) all-reduce(f32[768]{0:T(1024)S(1)} %get-tuple-element.738, ...), channel_id=3, replica_groups=mesh['dp'=4,'seq'=8] {'dp','seq'}, use_global_device_ids=true, to_apply=%region_25.26.clone | all-reduce | flops 9216 | bytes 73728
  662.5 4.2 convolution_add_fusion.3
  666.7 98.8 %reduce-scatter.9.cloned.1.call-done = f32[24,3072]{1,0:T(8,128)} async-done(((f32[768,3072]{1,0:T(8,128)}), f32[24,3072]{1,0:T(8,128)}) %reduce-scatter.9.cloned.1.call-update) | async-done | bytes 294928 | tf_op jit(solution)/shard_map/reduce_scatter | solution.py:334
  765.4 141.2 %reduce-scatter.11.cloned.1.call-done = f32[96,768]{1,0:T(8,128)} async-done(((f32[3072,768]{1,0:T(8,128)}), f32[96,768]{1,0:T(8,128)}) %reduce-scatter.11.cloned.1.call-update) | async-done | bytes 294928 | tf_op jit(solution)/shard_map/reduce_scatter | solution.py:336
  906.7 125.3 %reduce-scatter.13.cloned.1.call-done = f32[24,2304]{1,0:T(8,128)} async-done(((f32[768,2304]{1,0:T(8,128)}), f32[24,2304]{1,0:T(8,128)}) %reduce-scatter.13.cloned.1.call-update) | async-done | bytes 221200
  (361 shorter events, 140.9 us)
Async XLA Ops:
  7.2 66.8 %all-gather.9.cloned.1.call-start = ((), (), s32[]{:S(2)}) async-start(), calls=%async_computation.4 | async-start | bytes 3649536 | tf_op jit(solution)/shard_map/all_gather | solution.py:196
  7.9 132.4 %all-gather.11.cloned.1.call-start = ((), (), s32[]{:S(2)}) async-start(), calls=%async_computation.5 | async-start | bytes 3538944 | tf_op jit(solution)/shard_map/all_gather | solution.py:227
  77.2 8.0 copy-start.14
  78.3 125.3 %all-gather.13.cloned.1.call-start = ((), (), s32[]{:S(2)}) async-start(), calls=%async_computation.6 | async-start | bytes 3538944 | tf_op jit(solution)/shard_map/all_gather | solution.py:228
  79.3 179.6 %all-gather.15.cloned.1.call-start = ((), (), s32[]{:S(2)}) async-start(), calls=%async_computation.7 | async-start | bytes 1216512 | tf_op jit(solution)/shard_map/all_gather | solution.py:199
  79.9 244.5 %all-gather.17.cloned.1.call-start = ((), (), s32[]{:S(2)}) async-start(), calls=%async_computation.8 | async-start | bytes 4866048 | tf_op jit(solution)/shard_map/all_gather | solution.py:203
  80.4 309.3 %all-gather.19.cloned.1.call-start = ((), (), s32[]{:S(2)}) async-start(), calls=%async_computation.9 | async-start | bytes 4866048 | tf_op jit(solution)/shard_map/all_gather | solution.py:205
  81.0 442.0 %all-gather.21.cloned.1.call-start = ((), (), s32[]{:S(2)}) async-start(), calls=%async_computation.10 | async-start | bytes 3538944 | tf_op jit(solution)/shard_map/all_gather | solution.py:302
  85.3 119.0 %copy-start.25 = (s32[2,128]{1,0:T(2,128)}, s32[2,128]{1,0:T(2,128)S(1)}, u32[]{:S(2)}) copy-start(s32[2,128]{1,0:T(2,128)S(1)} %constant_dynamic-slice_fusion.14) | copy-start | bytes 3076
  87.2 435.9 %all-gather.23.cloned.1.call-start = ((), (), s32[]{:S(2)}) async-start(), calls=%async_computation.11 | async-start | bytes 3538944 | tf_op jit(solution)/shard_map/all_gather | solution.py:303
  204.2 54.6 %copy-start.8 = (bf16[2,128,768]{2,1,0:T(8,128)(2,1)S(1)}, bf16[2,128,768]{2,1,0:T(8,128)(2,1)}, u32[]{:S(2)}) copy-start(bf16[2,128,768]{2,1,0:T(8,128)(2,1)} %param.28) | copy-start | bytes 1179652
  238.4 85.9 %copy-start.12 = (f32[768]{0:T(1024)S(1)}, f32[768]{0:T(1024)}, u32[]{:S(2)}) copy-start(f32[768]{0:T(1024)} %convert_element_type.128) | copy-start | bytes 9220
  238.5 85.9 %copy-start.13 = (f32[768]{0:T(1024)S(1)}, f32[768]{0:T(1024)}, u32[]{:S(2)}) copy-start(f32[768]{0:T(1024)} %convert_element_type.129) | copy-start | bytes 9220
  238.5 85.9 %copy-start.23 = (f32[3072]{0:T(1024)S(1)}, f32[3072]{0:T(1024)}, u32[]{:S(2)}) copy-start(f32[3072]{0:T(1024)} %convert_element_type.131) | copy-start | bytes 36868
  261.0 140.9 %copy-start.21 = (f32[256]{0:T(256)}, f32[256]{0:T(256)S(1)}, u32[]{:S(2)}) copy-start(f32[256]{0:T(256)S(1)} %fusion.25) | copy-start | bytes 3076
  261.0 128.7 %copy-start.27 = (f32[768]{0:T(1024)S(1)}, f32[768]{0:T(1024)}, u32[]{:S(2)}) copy-start(f32[768]{0:T(1024)} %convert_element_type.133) | copy-start | bytes 9220
  389.7 7.1 slice-start.2
  389.7 4.3 copy-start.4
  389.7 4.3 copy-start.16
  389.7 5.3 copy-start.17
  389.7 7.1 slice-start.3
  389.7 7.1 copy-start.33
  393.7 3.1 copy-start.32
  396.1 3.5 slice-start
  396.9 2.8 slice-start.1
  399.6 2.3 copy-start.10
  401.9 1.3 copy-start
  401.9 4.5 copy-start.9
  402.3 2.1 copy-start.6
  402.3 2.1 copy-start.30
  406.3 2.1 copy-start.22
  406.4 260.3 %reduce-scatter.7.cloned.1.call-start = ((), (), s32[]{:S(2)}) async-start(), calls=%async_computation.12 | async-start | bytes 2433024 | tf_op jit(solution)/shard_map/reduce_scatter | solution.py:330
  408.3 357.1 %reduce-scatter.9.cloned.1.call-start = ((), (), s32[]{:S(2)}) async-start(), calls=%async_computation.13 | async-start | bytes 9732096 | tf_op jit(solution)/shard_map/reduce_scatter | solution.py:334
  415.0 1.7 copy-start.11
  415.1 491.6 %reduce-scatter.11.cloned.1.call-start = ((), (), s32[]{:S(2)}) async-start(), calls=%async_computation.14 | async-start | bytes 9732096 | tf_op jit(solution)/shard_map/reduce_scatter | solution.py:336
  490.1 541.9 %reduce-scatter.13.cloned.1.call-start = ((), (), s32[]{:S(2)}) async-start(), calls=%async_computation.15 | async-start | bytes 7299072
  615.3 1.0 copy-start.5
  615.3 1.1 copy-start.1
  615.3 1.2 copy-start.2
  615.3 1.4 copy-start.3
  615.4 2.1 copy-start.18
  615.4 2.1 copy-start.19
  615.4 2.1 copy-start.20
  615.4 2.1 copy-start.24
  615.4 2.1 copy-start.28
  615.4 2.1 copy-start.29
  615.4 47.1 %copy-start.7 = (f32[256,768]{1,0:T(8,128)S(1)}, f32[256,768]{1,0:T(8,128)}, u32[]{:S(2)}) copy-start(f32[256,768]{1,0:T(8,128)} %copy-done.6) | copy-start | bytes 2359300
  615.4 47.1 %copy-start.31 = (f32[256]{0:T(256)S(1)}, f32[256]{0:T(256)}, u32[]{:S(2)}) copy-start(f32[256]{0:T(256)} %copy-done.30) | copy-start | bytes 3076
  (2 other events, 1.4 us)
Sparse Core Ops, SparseCore 0:
  11.0 62.9 all-gather.8
  78.4 61.8 all-gather.10
  142.3 61.2 all-gather.12
  206.5 52.3 all-gather.14
  261.7 62.6 all-gather.16
  327.2 62.4 all-gather.18
  391.7 63.5 all-gather.20
  457.4 63.1 all-gather.22
  526.5 96.9 reduce-scatter.6
  630.8 134.5 reduce-scatter.8
  771.9 134.7 reduce-scatter.10
  913.7 118.1 reduce-scatter.12
where the time goes:
time: 1040 us
  waiting for transfers between devices  637 us (61%)
  blocking collectives  148 us (14%)
  local copies, waits for them, and re-layouts  128 us (12%)
  matrix products  93.9 us (9%)
  between operations  14.6 us (1%)
  other arithmetic  14.4 us (1%)
    reduce_scatter x1, waiting for transfers between devices, on_device(): lax.psum_scatter(grad_w_down, ('dp', 'seq'), scatter_dimension=0, tiled=T...  141 us
    unnamed x13, waiting for transfers between devices  128 us
    reduce_scatter x1, waiting for transfers between devices, on_device(): lax.psum_scatter(grad_w_up, ('dp', 'seq'), scatter_dimension=0, tiled=True)  98.8 us
    unnamed x2, blocking collectives  82.3 us
    all_gather x1, waiting for transfers between devices, on_device(): lax.all_gather(value_low, 'seq', axis=1, tiled=True)  63.3 us
    all_gather x1, waiting for transfers between devices, on_device(): lax.all_gather(w_up, ('dp', 'seq'), axis=0, tiled=True)  63.3 us
    all_gather x1, waiting for transfers between devices, on_device(): lax.all_gather(w_down, ('dp', 'seq'), axis=0, tiled=True)  54 us
    all_gather x1, waiting for transfers between devices, on_device(): lax.all_gather(key_low, 'seq', axis=1, tiled=True)  52.9 us
  transfers between devices with their start and end apart: 12, of which 9 were waited for; matrix products, arithmetic and copies ran while one was open for 22% of the time, Pallas kernels for 0%

commit v1 on v0

--- a/solution.py
+++ b/solution.py
@@ -1,6 +1,8 @@
 import jax
 import jax.numpy as jnp
 from jax import lax
+from jax.experimental import pallas as pl
+from jax.experimental.pallas import tpu as pltpu
 from jax.sharding import PartitionSpec as P
 
 HEAD = 64
@@ -174,7 +176,7 @@
     return lax.fori_loop(0, groups, one_group, start_state)
 
 
-def on_device(
+def on_device_general(
     tokens,
     segments,
     cotangent,
@@ -343,7 +345,296 @@
     return (final_out, grad_tokens) + tuple(owned)
 
 
+def forward_kernel(q_ref, k_ref, v_ref, row_doc, col_doc, out_ref, log_ref):
+    scores = contract_cols(q_ref[0], k_ref[0]) * HEAD ** (-0.5)
+    scores = jnp.where(row_doc[...] == col_doc[...], scores, masked_out)
+    highest = jnp.max(scores, axis=1, keepdims=True)
+    exponent = jnp.exp(scores - highest)
+    denominator = jnp.sum(exponent, axis=1, keepdims=True)
+    weights = (exponent * (1.0 / denominator)).astype(jnp.bfloat16)
+    out_ref[0] = jnp.dot(weights, v_ref[0], preferred_element_type=jnp.float32).astype(jnp.bfloat16)
+    log_ref[0] = highest + jnp.log(denominator)
+
+
+def backward_kernel(q_ref, k_ref, v_ref, g_ref, log_ref, row_doc, col_doc, dq_ref, dk_ref, dv_ref):
+    queries, keys, grads = q_ref[0], k_ref[0], g_ref[0]
+    scores = contract_cols(queries, keys) * HEAD ** (-0.5)
+    scores = jnp.where(row_doc[...] == col_doc[...], scores, masked_out)
+    probs = jnp.exp(scores - log_ref[0])
+    grad_probs = contract_cols(grads, v_ref[0])
+    row_delta = jnp.sum(probs * grad_probs, axis=1, keepdims=True)
+    grad_scores = (probs * (grad_probs - row_delta)).astype(jnp.bfloat16)
+    dq_ref[0] = jnp.dot(grad_scores, keys, preferred_element_type=jnp.float32) * HEAD ** (-0.5)
+    key_term = contract_rows(grad_scores, queries) * HEAD ** (-0.5)
+    value_term = contract_rows(probs.astype(jnp.bfloat16), grads)
+
+    @pl.when(pl.program_id(1) == 0)
+    def _():
+        dk_ref[0] = key_term
+        dv_ref[0] = value_term
+
+    @pl.when(pl.program_id(1) != 0)
+    def _():
+        dk_ref[0] += key_term
+        dv_ref[0] += value_term
+
+
+def attention_specs(heads, length, rows):
+    own = pl.BlockSpec((1, rows, HEAD), lambda h, r: (h, r, 0))
+    full = pl.BlockSpec((1, length, HEAD), lambda h, r: (h, 0, 0))
+    column = pl.BlockSpec((1, rows, 1), lambda h, r: (h, r, 0))
+    row_doc = pl.BlockSpec((rows, 1), lambda h, r: (r, 0))
+    col_doc = pl.BlockSpec((1, length), lambda h, r: (0, 0))
+    return own, full, column, row_doc, col_doc
+
+
+def local_forward(queries, keys, values, docs):
+    heads, length, _ = queries.shape
+    rows = min(256, length)
+    own, full, column, row_doc, col_doc = attention_specs(heads, length, rows)
+    return pl.pallas_call(
+        forward_kernel,
+        grid=(heads, length // rows),
+        in_specs=[own, full, full, row_doc, col_doc],
+        out_specs=[own, column],
+        out_shape=[
+            jax.ShapeDtypeStruct((heads, length, HEAD), jnp.bfloat16),
+            jax.ShapeDtypeStruct((heads, length, 1), jnp.float32),
+        ],
+        compiler_params=pltpu.CompilerParams(vmem_limit_bytes=40 * 1024 * 1024),
+        cost_estimate=pl.CostEstimate(
+            flops=16 * heads * length * length * HEAD,
+            bytes_accessed=8 * heads * length * HEAD,
+            transcendentals=heads * length * length,
+        ),
+    )(queries, keys, values, docs[:, None], docs[None, :])
+
+
+def local_backward(queries, keys, values, grads, log_sums, docs):
+    heads, length, _ = queries.shape
+    rows = min(256, length)
+    own, full, column, row_doc, col_doc = attention_specs(heads, length, rows)
+    shape = jax.ShapeDtypeStruct((heads, length, HEAD), jnp.float32)
+    return pl.pallas_call(
+        backward_kernel,
+        grid=(heads, length // rows),
+        in_specs=[own, full, full, own, column, row_doc, col_doc],
+        out_specs=[own, full, full],
+        out_shape=[shape] * 3,
+        compiler_params=pltpu.CompilerParams(vmem_limit_bytes=40 * 1024 * 1024),
+        cost_estimate=pl.CostEstimate(
+            flops=40 * heads * length * length * HEAD,
+            bytes_accessed=20 * heads * length * HEAD,
+            transcendentals=heads * length * length,
+        ),
+    )(queries, keys, values, grads, log_sums, docs[:, None], docs[None, :])
+
+
+def on_device_packed(
+    devices,
+    ring,
+    tokens,
+    segments,
+    cotangent,
+    w_qkv,
+    bias_q,
+    bias_v,
+    w_out,
+    bias_out,
+    gain_one,
+    shift_one,
+    w_up,
+    bias_up,
+    w_down,
+    bias_down,
+    gain_two,
+    shift_two,
+):
+    both = ("dp", "seq")
+    seq_count, slice_len, model_width = tokens.shape
+    row_total = seq_count * slice_len
+    own_rows = w_qkv.shape[0]
+    fold = w_up.shape[1] // model_width
+    down_rows = w_down.shape[0]
+    vectors = (bias_q, bias_v, bias_out, gain_one, shift_one, bias_down, gain_two, shift_two)
+    count = len(vectors)
+    qkv_width = 3 * model_width
+
+    rest = jnp.concatenate(
+        [w_down, w_out] + [w_up[:, i * model_width : (i + 1) * model_width] for i in range(fold)],
+        axis=0,
+    )
+    rest_all = lax.all_gather(rest, both, axis=0, tiled=False)
+    extra = jnp.concatenate(
+        [jnp.stack(vectors, axis=1), bias_up.reshape(own_rows, fold)], axis=1
+    )
+    first = jnp.concatenate(
+        [w_qkv, jnp.pad(extra, ((0, 0), (0, 128 - count - fold)))], axis=1
+    )
+    first_all = lax.all_to_all(
+        jnp.broadcast_to(first[None], (devices,) + first.shape), both, 0, 0, tiled=True
+    ).reshape(devices * own_rows, qkv_width + 128)
+    w_qkv_all = first_all[:, :qkv_width]
+    small = first_all[:, qkv_width : qkv_width + count + fold].astype(jnp.float32)
+    bq, bv, bo, g1, s1, bd, g2, s2 = [small[:, i] for i in range(count)]
+    bu = small[:, count:].reshape(-1)
+
+    inputs = tokens.reshape(row_total, model_width)
+    qkv_bias = jnp.concatenate([bq, jnp.zeros((model_width,), jnp.float32), bv])
+    projected = (
+        jnp.dot(inputs, w_qkv_all, preferred_element_type=jnp.float32) + qkv_bias
+    ).astype(jnp.bfloat16)
+
+    groups = ring // seq_count
+    width = model_width // groups
+    heads = width // HEAD
+    length = ring * slice_len
+    sent = projected.reshape(seq_count, slice_len, 3, groups, width)
+    sent = sent.transpose(0, 3, 1, 2, 4).reshape(ring, slice_len, 3 * width)
+    own = lax.all_to_all(sent, "seq", 0, 0, tiled=True).reshape(length, 3, heads, HEAD)
+    own = own.transpose(1, 2, 0, 3)
+    own_seq = lax.axis_index("seq") // groups
+    docs = lax.dynamic_index_in_dim(segments, own_seq, 0, keepdims=False)
+    mixed_own, log_sums = local_forward(own[0], own[1], own[2], docs)
+    mixed_sent = mixed_own.transpose(1, 0, 2).reshape(ring, slice_len, width)
+    mixed = lax.all_to_all(mixed_sent, "seq", 0, 0, tiled=True)
+    mixed_low = (
+        mixed.reshape(seq_count, groups, slice_len, width)
+        .transpose(0, 2, 1, 3)
+        .reshape(row_total, model_width)
+    )
+
+    w_down_all = rest_all[:, :down_rows].reshape(-1, model_width)
+    w_out_all = rest_all[:, down_rows : down_rows + own_rows].reshape(-1, model_width)
+    up_start = down_rows + own_rows
+    w_up_all = jnp.concatenate(
+        [
+            rest_all[:, up_start + i * own_rows : up_start + (i + 1) * own_rows].reshape(
+                -1, model_width
+            )
+            for i in range(fold)
+        ],
+        axis=1,
+    )
+    branch = jnp.dot(mixed_low, w_out_all, preferred_element_type=jnp.float32) + bo
+    normed_one, norm_one_back = jax.vjp(normalize, inputs.astype(jnp.float32) + branch, g1, s1)
+    normed_low = normed_one.astype(jnp.bfloat16)
+    hidden = jnp.dot(normed_low, w_up_all, preferred_element_type=jnp.float32) + bu
+    activated, gelu_back = jax.vjp(exact_gelu, hidden)
+    activated_low = activated.astype(jnp.bfloat16)
+    feed = jnp.dot(activated_low, w_down_all, preferred_element_type=jnp.float32) + bd
+    result, norm_two_back = jax.vjp(normalize, normed_one + feed, g2, s2)
+
+    grad_sum_two, grad_gain_two, grad_shift_two = norm_two_back(
+        cotangent.reshape(row_total, model_width).astype(jnp.float32)
+    )
+    grad_feed = grad_sum_two.astype(jnp.bfloat16)
+    grad_w_down = contract_rows(activated_low, grad_feed).astype(jnp.bfloat16)
+    grad_bias_down = column_sum(grad_feed)
+    (grad_hidden,) = gelu_back(contract_cols(grad_feed, w_down_all))
+    grad_hidden_low = grad_hidden.astype(jnp.bfloat16)
+    grad_w_up = contract_rows(normed_low, grad_hidden_low).astype(jnp.bfloat16)
+    grad_bias_up = column_sum(grad_hidden_low)
+    grad_normed = grad_sum_two + contract_cols(grad_hidden_low, w_up_all)
+    grad_sum_one, grad_gain_one, grad_shift_one = norm_one_back(grad_normed)
+    grad_branch = grad_sum_one.astype(jnp.bfloat16)
+    grad_w_out = contract_rows(mixed_low, grad_branch).astype(jnp.bfloat16)
+    grad_bias_out = column_sum(grad_branch)
+
+    packed = jnp.concatenate(
+        [
+            grad_w_down.reshape(devices, down_rows, model_width),
+            grad_w_out.reshape(devices, own_rows, model_width),
+        ]
+        + [
+            grad_w_up[:, i * model_width : (i + 1) * model_width].reshape(
+                devices, own_rows, model_width
+            )
+            for i in range(fold)
+        ],
+        axis=1,
+    )
+    rest_sum = lax.psum_scatter(
+        packed.reshape(-1, model_width), both, scatter_dimension=0, tiled=True
+    ).astype(jnp.float32)
+
+    grad_mixed = contract_cols(grad_branch, w_out_all).astype(jnp.bfloat16)
+    grad_sent = (
+        grad_mixed.reshape(seq_count, slice_len, groups, width)
+        .transpose(0, 2, 1, 3)
+        .reshape(ring, slice_len, width)
+    )
+    grad_own = lax.all_to_all(grad_sent, "seq", 0, 0, tiled=True)
+    grad_own = grad_own.reshape(length, heads, HEAD).transpose(1, 0, 2)
+    parts = local_backward(own[0], own[1], own[2], grad_own, log_sums, docs)
+    back = jnp.stack(parts).astype(jnp.bfloat16)
+    back = back.transpose(2, 0, 1, 3).reshape(ring, slice_len, 3 * width)
+    back = lax.all_to_all(back, "seq", 0, 0, tiled=True)
+    grad_proj = (
+        back.reshape(seq_count, groups, slice_len, 3, width)
+        .transpose(0, 2, 3, 1, 4)
+        .reshape(row_total, qkv_width)
+    )
+    grad_w_qkv = contract_rows(inputs, grad_proj)
+    grad_bias_q = column_sum(grad_proj[:, :model_width])
+    grad_bias_v = column_sum(grad_proj[:, 2 * model_width :])
+    grad_inputs = grad_sum_one + contract_cols(grad_proj, w_qkv_all)
+
+    grads = (
+        grad_bias_q,
+        grad_bias_v,
+        grad_bias_out,
+        grad_gain_one,
+        grad_shift_one,
+        grad_bias_down,
+        grad_gain_two,
+        grad_shift_two,
+    )
+    extra = jnp.concatenate(
+        [jnp.stack(grads, axis=1), grad_bias_up.reshape(-1, fold)], axis=1
+    )
+    last = jnp.concatenate(
+        [grad_w_qkv, jnp.pad(extra, ((0, 0), (0, 128 - count - fold)))], axis=1
+    ).astype(jnp.bfloat16)
+    last = lax.all_to_all(
+        last.reshape(devices, own_rows, qkv_width + 128), both, 0, 0, tiled=True
+    )
+    last = jnp.sum(last.astype(jnp.float32), axis=0)
+    sums = [last[:, qkv_width + i] for i in range(count)]
+    own_up = jnp.concatenate(
+        [rest_sum[up_start + i * own_rows : up_start + (i + 1) * own_rows] for i in range(fold)],
+        axis=1,
+    )
+    return (
+        result.astype(jnp.bfloat16).reshape(seq_count, slice_len, model_width),
+        grad_inputs.reshape(seq_count, slice_len, model_width),
+        last[:, :qkv_width],
+        sums[0],
+        sums[1],
+        rest_sum[down_rows : down_rows + own_rows],
+        sums[2],
+        sums[3],
+        sums[4],
+        own_up,
+        last[:, qkv_width + count : qkv_width + count + fold].reshape(-1),
+        rest_sum[:down_rows],
+        sums[5],
+        sums[6],
+        sums[7],
+    )
+
+
 def solution(mesh):
+    ring = mesh.shape["seq"]
+    devices = ring * mesh.shape["dp"]
+
+    def on_device(*arguments):
+        seq_count, _, model_width = arguments[0].shape
+        heads = model_width // HEAD
+        if ring % seq_count == 0 and heads % (ring // seq_count) == 0:
+            return on_device_packed(devices, ring, *arguments)
+        return on_device_general(*arguments)
+
     return jax.shard_map(
         on_device,
         mesh=mesh,

time: 1040 us -> 507 us (0.49)
  waiting for transfers between devices: 637 us -> 190 us
  local copies, waits for them, and re-layouts: 128 us -> 60.8 us
  matrix products: 93.9 us -> 27.2 us
  Pallas kernels: 0 us -> 25.6 us
  starting transfers between devices: 0.66 us -> 14.9 us
    all_gather x8 -> x1, waiting for transfers between devices: 270 us -> 0.01 us  [on_device_packed(): rest_all = lax.all_gather(rest, both, axis=0, tiled=False)]
    reduce_scatter x3 -> x1, waiting for transfers between devices: 240 us -> 0.01 us  [on_device_packed(): lax.psum_scatter(packed.reshape(-1, model_width), both, scatter_dimension...]
    all_to_all x0 -> x4, waiting for transfers between devices: none -> 190 us  [the longest x1 103 us: on_device_packed(): lax.all_to_all(last.reshape(devices, own_rows, qkv_width + 128), both, 0,...]
    all_to_all x0 -> x2, blocking collectives: none -> 155 us  [the longest x1 140 us: on_device_packed(): lax.all_to_all(jnp.broadcast_to(first[None], (devices,) + first.shape), b...]
    unnamed x13 -> x2, waiting for transfers between devices: 128 us -> 0.03 us
    unnamed x2 -> x0, blocking collectives: 82.3 us -> none
    all_gather x2 -> x0, blocking collectives: 66.2 us -> none  [the longest x1 33.3 us: on_device(): lax.all_gather(log_sums, 'seq', axis=2, tiled=True)]
    dot_general x52 -> x4, matrix products: 64.6 us -> 11.2 us  [the longest x1 7.79 us: on_device_packed(): jnp.dot(normed_low, w_up_all, preferred_element_type=jnp.float32) + bu]
  transfers between devices with their start and end apart: 12 -> 6, of which waited for: 9 -> 4; matrix products, arithmetic and copies ran while one was open for 22% -> 10% of each run, Pallas kernels for 0% -> 5%
where the time goes in v1:
time: 507 us; the launch traced here: 501 us
  waiting for transfers between devices  190 us (37%)
  blocking collectives  155 us (31%)
  local copies, waits for them, and re-layouts  60.8 us (12%)
  matrix products  27.2 us (5%)
  Pallas kernels  25.6 us (5%)
  between operations  15.3 us (3%)
  starting transfers between devices  14.9 us (3%)
  other arithmetic  11.1 us (2%)
    all_to_all x1, blocking collectives, on_device_packed(): lax.all_to_all(jnp.broadcast_to(first[None], (devices,) + first.shape), b...  140 us
    all_to_all x1, waiting for transfers between devices, on_device_packed(): lax.all_to_all(last.reshape(devices, own_rows, qkv_width + 128), both, 0,...  103 us
    all_to_all x1, waiting for transfers between devices, on_device_packed(): back = lax.all_to_all(back, 'seq', 0, 0, tiled=True)  49.8 us
    all_to_all x1, waiting for transfers between devices, on_device_packed(): lax.all_to_all(sent, 'seq', 0, 0, tiled=True)  27.2 us
    unnamed x73, local copies, waits for them, and re-layouts  17.4 us
    all_to_all x1, blocking collectives, on_device_packed(): grad_own = lax.all_to_all(grad_sent, 'seq', 0, 0, tiled=True)  15.8 us
    pallas_call x1, Pallas kernels, local_backward(): pl.pallas_call(backward_kernel, grid=(heads, length // rows), in_specs=[o...  15.6 us
    dot_general x4, matrix products, contract_cols(): lax.dot_general(first_op, second_op, (((1,), (1,)), ((), ())), preferred_...  11.3 us
  transfers between devices with their start and end apart: 6, of which 4 were waited for; matrix products, arithmetic and copies ran while one was open for 10% of the time, Pallas kernels for 5%

profile of v1, /device:TPU:0, one launch (start us, length us, event | category | flops | bytes accessed | tf_op | source)
XLA Modules:
  0.0 500.7 jit_solution(11931311231040811833)
XLA Ops:
  20.8 139.6 %all_to_all.30 = bf16[32,24,2432]{2,1,0:T(8,128)(2,1)S(1)} all-to-all(bf16[32,24,2432]{2,1,0:T(8,128)(2,1)S(1)} %broadcast_in_dim.14), channel_id=1, replica_groups=mesh['dp'=4,'seq'=8] {'dp','seq'}, dimensions={0} | all-to-all | bytes 7471104 | tf_op jit(solution)/shard_map/all_to_all | solution.py:474
  160.5 2.1 slice_reduce_fusion.3
  162.6 1.3 fusion.1
  164.3 1.3 copy.159
  165.6 3.6 all-to-all-start.1
  169.2 1.0 copy.162.row_doc
  170.2 27.2 %all-to-all-done.1 = bf16[8,128,576]{1,2,0:T(8,128)(2,1)S(1)} async-done(((bf16[8,128,576]{1,2,0:T(8,128)(2,1)}), bf16[8,128,576]{1,2,0:T(8,128)(2,1)S(1)}, u32[]{:S(2)}, u32[]{:S(2)}) %all-to-all-start.1) | async-done | bytes 1179680 | tf_op jit(solution)/shard_map/all_to_all | solution.py:494
  198.7 2.4 copy.161
  201.2 1.8 slice_bitcast_fusion
  203.0 9.9 %shard_map.271 = (bf16[3,1024,64]{2,1,0:T(8,128)(2,1)S(1)}, f32[3,1024,1]{2,1,0:T(8,128)S(1)}) custom-call(bf16[3,1024,64]{2,1,0:T(8,128)(2,1)S(1)} %get-tuple-element.71.q_ref, bf16[3,1024,64]{2,1,0:T(8,128)(2,1)S(1)} %get-tuple-element.70.k_ref, bf16[3,1024,64]{2,1,0:T(8,128)(2,1)S(1)} %get-tuple-element.69.v_ref, s32[1024,1]{1,0:T(8,128)S(1)} %copy-done.2, ...), custom_call_target="tpu_custom_call" | custom-call | flops 3221225472 | bytes 1572864 | tf_op jit(solution)/shard_map/pallas_call | solution.py:395
  212.9 1.1 copy-done.4
  215.1 1.1 copy.182
  216.9 3.5 all-to-all-start.2
  221.7 10.7 %all-to-all-done.2 = bf16[8,128,192]{1,2,0:T(8,128)(2,1)S(1)} async-done(((bf16[8,128,192]{1,2,0:T(8,128)(2,1)}), bf16[8,128,192]{1,2,0:T(8,128)(2,1)S(1)}, u32[]{:S(2)}, u32[]{:S(2)}) %all-to-all-start.2) | async-done | bytes 393248 | tf_op jit(solution)/shard_map/all_to_all | solution.py:500
  232.4 1.2 copy.165
  233.5 2.6 slice.203
  236.2 3.2 fusion.39
  240.3 7.8 %multiply_convert_fusion = (bf16[256,3072]{1,0:T(8,128)(2,1)S(1)}, f32[256,3072]{1,0:T(8,128)S(1)}, f32[256,3072]{1,0:T(8,128)S(1)}) fusion(f32[3072]{0:T(1024)S(1)} %copy-done.21, bf16[768,768]{1,0:T(8,128)(2,1)S(1)} %bitcast.153, bf16[768,768]{1,0:T(8,128)(2,1)S(1)} %bitcast.155, bf16[768,768]{1,0:T(8,128)(2,1)S(1)} %bitcast.157, ...), kind=kOutput, calls=%fused_computation.13 | convolution fusion | flops 1279721472 | bytes 13389824 | tf_op jit(solution)/shard_map/dot_general | solution.py:522
  248.1 1.5 fusion.43
  250.8 1.3 fusion.37
  252.3 2.8 fusion.33
  255.1 2.2 multiply_reduce_fusion
  257.3 1.6 convolution_convert_fusion
  258.9 1.4 convolution_convert_fusion.1
  261.8 2.6 constant_dynamic-update-slice_fusion.7
  264.4 1.1 constant_dynamic-update-slice_fusion.6
  265.5 1.2 constant_dynamic-update-slice_fusion.5
  266.7 1.1 constant_dynamic-update-slice_fusion.4
  267.8 1.1 constant_dynamic-update-slice_fusion.3
  268.9 1.1 constant_dynamic-update-slice_fusion.2
  270.0 2.3 convolution_convert_fusion.4
  272.3 1.2 copy.166
  273.6 15.8 %all_to_all.31 = bf16[8,128,192]{1,2,0:T(8,128)(2,1)S(1)} all-to-all(bf16[8,128,192]{1,2,0:T(8,128)(2,1)S(1)} %bitcast.149), channel_id=1, replica_groups=mesh['dp'=4,'seq'=8] {'seq'}, dimensions={0} | all-to-all | bytes 786432 | tf_op jit(solution)/shard_map/all_to_all | solution.py:567
  290.3 1.1 copy-done.3
  291.4 1.5 copy-done.5
  292.9 15.6 %shard_map.272 = (f32[3,1024,64]{2,1,0:T(8,128)S(1)}, f32[3,1024,64]{2,1,0:T(8,128)S(1)}, f32[3,1024,64]{2,1,0:T(8,128)S(1)}) custom-call(bf16[3,1024,64]{2,1,0:T(8,128)(2,1)S(1)} %get-tuple-element.71.q_ref, bf16[3,1024,64]{2,1,0:T(8,128)(2,1)S(1)} %get-tuple-element.70.k_ref, bf16[3,1024,64]{2,1,0:T(8,128)(2,1)S(1)} %get-tuple-element.69.v_ref, ...), custom_call_target="tpu_custom_call" | custom-call | flops 8053063680 | bytes 3932160 | tf_op jit(solution)/shard_map/pallas_call | solution.py:418
  310.8 1.2 copy.172
  312.0 3.6 all-to-all-start.4
  317.9 49.8 %all-to-all-done.4 = bf16[8,128,576]{1,2,0:T(8,128)(2,1)S(1)} async-done(((bf16[8,128,576]{1,2,0:T(8,128)(2,1)}), bf16[8,128,576]{1,2,0:T(8,128)(2,1)S(1)}, u32[]{:S(2)}, u32[]{:S(2)}) %all-to-all-start.4) | async-done | bytes 1179680 | tf_op jit(solution)/shard_map/all_to_all | solution.py:572
  367.7 1.2 copy.173
  370.7 1.1 convolution_convert_fusion.2
  371.8 2.1 pad_maximum_fusion.1
  373.9 4.0 all-to-all-start.5
  377.9 4.1 fusion.12
  382.0 102.7 %all-to-all-done.5 = bf16[32,24,2432]{2,1,0:T(8,128)(2,1)} async-done(((bf16[32,24,2432]{2,1,0:T(8,128)(2,1)}), bf16[32,24,2432]{2,1,0:T(8,128)(2,1)}, u32[]{:S(2)}, u32[]{:S(2)}) %all-to-all-start.5) | async-done | bytes 3735584 | tf_op jit(solution)/shard_map/all_to_all | solution.py:599
  484.7 2.6 convert_reduce_fusion
  489.5 1.5 fusion.41
  491.7 1.6 slice.225
  (139 shorter events, 31.9 us)
Async XLA Ops:
  7.2 162.0 %copy-start = (s32[2,1024]{1,0:T(2,128)S(1)}, s32[2,1024]{1,0:T(2,128)}, u32[]{:S(2)}) copy-start(s32[2,1024]{1,0:T(2,128)} %param.17) | copy-start | bytes 24580
  7.2 226.3 %all-gather.3.cloned.1.call-start = ((), (), s32[]{:S(2)}) async-start(), calls=%async_computation.8 | async-start | bytes 10948608 | tf_op jit(solution)/shard_map/all_gather | solution.py:467
  12.0 0.7 copy-start.14
  160.4 2.2 copy-start.6
  160.5 2.2 copy-start.15
  165.6 31.8 %all-to-all-start.1 = ((bf16[8,128,576]{1,2,0:T(8,128)(2,1)}), bf16[8,128,576]{1,2,0:T(8,128)(2,1)S(1)}, u32[]{:S(2)}, u32[]{:S(2)}) async-start(bf16[8,128,576]{1,2,0:T(8,128)(2,1)} %bitcast.12), calls=%async_computation.1 | async-start | bytes 2359296 | tf_op jit(solution)/shard_map/all_to_all | solution.py:494
  201.2 1.8 copy-start.2
  212.9 1.1 copy-start.4
  216.9 15.4 %all-to-all-start.2 = ((bf16[8,128,192]{1,2,0:T(8,128)(2,1)}), bf16[8,128,192]{1,2,0:T(8,128)(2,1)S(1)}, u32[]{:S(2)}, u32[]{:S(2)}) async-start(bf16[8,128,192]{1,2,0:T(8,128)(2,1)} %copy.164), calls=%async_computation.2 | async-start | bytes 786432 | tf_op jit(solution)/shard_map/all_to_all | solution.py:500
  220.5 269.0 %reduce-scatter.2.cloned.1.call-start = ((), (), s32[]{:S(2)}) async-start(), calls=%async_computation.7 | async-start | bytes 10948608 | tf_op jit(solution)/shard_map/reduce_scatter | solution.py:557
  236.2 3.2 copy-start.12
  236.2 3.2 copy-start.16
  236.2 3.2 copy-start.25
  239.3 0.9 copy-start.18
  239.4 0.9 copy-start.21
  240.3 7.8 %copy-start.24 = (f32[768]{0:T(1024)S(1)}, f32[768]{0:T(1024)}, u32[]{:S(2)}) copy-start(f32[768]{0:T(1024)} %get-tuple-element.34) | copy-start | bytes 9220
  248.1 1.8 copy-start.7
  248.1 1.8 copy-start.19
  248.1 2.7 copy-start.20
  260.7 1.0 copy-start.10
  260.8 1.0 copy-start.26
  260.9 0.8 copy-start.9
  290.3 1.1 copy-start.3
  291.4 1.5 copy-start.5
  310.4 5.1 %copy-start.8 = (bf16[2,128,768]{2,1,0:T(8,128)(2,1)S(1)}, bf16[2,128,768]{2,1,0:T(8,128)(2,1)}, u32[]{:S(2)}) copy-start(bf16[2,128,768]{2,1,0:T(8,128)(2,1)} %param.18) | copy-start | bytes 1179652
  310.8 5.1 %copy-start.22 = (bf16[768]{0:T(1024)(128)(2,1)S(1)}, bf16[768]{0:T(1024)(128)(2,1)}, u32[]{:S(2)}) copy-start(bf16[768]{0:T(1024)(128)(2,1)} %get-tuple-element.27) | copy-start | bytes 4612
  310.8 5.3 %copy-start.23 = (bf16[3072]{0:T(1024)(128)(2,1)S(1)}, bf16[3072]{0:T(1024)(128)(2,1)}, u32[]{:S(2)}) copy-start(bf16[3072]{0:T(1024)(128)(2,1)} %get-tuple-element.48) | copy-start | bytes 18436
  310.8 5.7 %copy-start.29 = (bf16[768]{0:T(1024)(128)(2,1)S(1)}, bf16[768]{0:T(1024)(128)(2,1)}, u32[]{:S(2)}) copy-start(bf16[768]{0:T(1024)(128)(2,1)} %get-tuple-element.25) | copy-start | bytes 4612
  310.8 6.0 %copy-start.28 = (bf16[768]{0:T(1024)(128)(2,1)S(1)}, bf16[768]{0:T(1024)(128)(2,1)}, u32[]{:S(2)}) copy-start(bf16[768]{0:T(1024)(128)(2,1)} %get-tuple-element.31) | copy-start | bytes 4612
  312.0 55.7 %all-to-all-start.4 = ((bf16[8,128,576]{1,2,0:T(8,128)(2,1)}), bf16[8,128,576]{1,2,0:T(8,128)(2,1)S(1)}, u32[]{:S(2)}, u32[]{:S(2)}) async-start(bf16[8,128,576]{1,2,0:T(8,128)(2,1)} %copy.172), calls=%async_computation.4 | async-start | bytes 2359296 | tf_op jit(solution)/shard_map/all_to_all | solution.py:572
  368.9 0.9 copy-start.13
  368.9 1.8 copy-start.17
  373.9 4.0 copy-start.11
  373.9 4.0 copy-start.27
  373.9 110.7 %all-to-all-start.5 = ((bf16[32,24,2432]{2,1,0:T(8,128)(2,1)}), bf16[32,24,2432]{2,1,0:T(8,128)(2,1)}, u32[]{:S(2)}, u32[]{:S(2)}) async-start(bf16[32,24,2432]{2,1,0:T(8,128)(2,1)} %pad_maximum_fusion.1), calls=%async_computation.5 | async-start | bytes 7471104 | tf_op jit(solution)/shard_map/all_to_all | solution.py:599
  377.9 115.5 %copy-start.1 = (s32[2,1024]{1,0:T(2,128)S(1)}, s32[2,1024]{1,0:T(2,128)}, u32[]{:S(2)}) copy-start(s32[2,1024]{1,0:T(2,128)} %param.17) | copy-start | bytes 24580
Sparse Core Ops, SparseCore 0:
  12.9 140.6 all-gather.2
  270.1 202.2 reduce-scatter.1

commit v2 on v1

--- a/solution.py
+++ b/solution.py
@@ -465,35 +465,56 @@
         axis=0,
     )
     rest_all = lax.all_gather(rest, both, axis=0, tiled=False)
-    extra = jnp.concatenate(
-        [jnp.stack(vectors, axis=1), bias_up.reshape(own_rows, fold)], axis=1
-    )
-    first = jnp.concatenate(
-        [w_qkv, jnp.pad(extra, ((0, 0), (0, 128 - count - fold)))], axis=1
-    )
-    first_all = lax.all_to_all(
-        jnp.broadcast_to(first[None], (devices,) + first.shape), both, 0, 0, tiled=True
-    ).reshape(devices * own_rows, qkv_width + 128)
-    w_qkv_all = first_all[:, :qkv_width]
-    small = first_all[:, qkv_width : qkv_width + count + fold].astype(jnp.float32)
-    bq, bv, bo, g1, s1, bd, g2, s2 = [small[:, i] for i in range(count)]
-    bu = small[:, count:].reshape(-1)
-
-    inputs = tokens.reshape(row_total, model_width)
-    qkv_bias = jnp.concatenate([bq, jnp.zeros((model_width,), jnp.float32), bv])
-    projected = (
-        jnp.dot(inputs, w_qkv_all, preferred_element_type=jnp.float32) + qkv_bias
-    ).astype(jnp.bfloat16)
-
     groups = ring // seq_count
     width = model_width // groups
     heads = width // HEAD
     length = ring * slice_len
-    sent = projected.reshape(seq_count, slice_len, 3, groups, width)
-    sent = sent.transpose(0, 3, 1, 2, 4).reshape(ring, slice_len, 3 * width)
-    own = lax.all_to_all(sent, "seq", 0, 0, tiled=True).reshape(length, 3, heads, HEAD)
-    own = own.transpose(1, 2, 0, 3)
-    own_seq = lax.axis_index("seq") // groups
+    extra = jnp.concatenate(
+        [jnp.stack(vectors, axis=1), bias_up.reshape(own_rows, fold)], axis=1
+    )
+    extra = jnp.pad(extra, ((0, 0), (0, 128 - count - fold)))
+    blocks = w_qkv.reshape(own_rows, 3, groups, width).transpose(2, 0, 1, 3)
+    first = jnp.concatenate(
+        [
+            blocks.reshape(groups, own_rows, 3 * width),
+            jnp.broadcast_to(extra[None], (groups,) + extra.shape),
+        ],
+        axis=2,
+    )
+    first = jnp.broadcast_to(
+        first[None], (devices // groups,) + first.shape
+    ).reshape(devices, own_rows, 3 * width + 128)
+    first_all = lax.all_to_all(first, both, 0, 0, tiled=True).reshape(
+        devices * own_rows, 3 * width + 128
+    )
+    w_qkv_own = first_all[:, : 3 * width]
+    small = first_all[:, 3 * width : 3 * width + count + fold].astype(jnp.float32)
+    bq, bv, bo, g1, s1, bd, g2, s2 = [small[:, i] for i in range(count)]
+    bu = small[:, count:].reshape(-1)
+
+    inputs = tokens.reshape(row_total, model_width)
+    seq_inputs = lax.all_to_all(
+        jnp.broadcast_to(
+            tokens[:, None], (seq_count, groups, slice_len, model_width)
+        ).reshape(ring, slice_len, model_width),
+        "seq",
+        0,
+        0,
+        tiled=True,
+    ).reshape(length, model_width)
+    place = lax.axis_index("seq")
+    own_seq, own_group = place // groups, place % groups
+    qkv_bias = jnp.concatenate(
+        [
+            lax.dynamic_slice_in_dim(bq, own_group * width, width, 0),
+            jnp.zeros((width,), jnp.float32),
+            lax.dynamic_slice_in_dim(bv, own_group * width, width, 0),
+        ]
+    )
+    projected = (
+        jnp.dot(seq_inputs, w_qkv_own, preferred_element_type=jnp.float32) + qkv_bias
+    ).astype(jnp.bfloat16)
+    own = projected.reshape(length, 3, heads, HEAD).transpose(1, 2, 0, 3)
     docs = lax.dynamic_index_in_dim(segments, own_seq, 0, keepdims=False)
     mixed_own, log_sums = local_forward(own[0], own[1], own[2], docs)
     mixed_sent = mixed_own.transpose(1, 0, 2).reshape(ring, slice_len, width)
@@ -567,22 +588,26 @@
     grad_own = lax.all_to_all(grad_sent, "seq", 0, 0, tiled=True)
     grad_own = grad_own.reshape(length, heads, HEAD).transpose(1, 0, 2)
     parts = local_backward(own[0], own[1], own[2], grad_own, log_sums, docs)
-    back = jnp.stack(parts).astype(jnp.bfloat16)
-    back = back.transpose(2, 0, 1, 3).reshape(ring, slice_len, 3 * width)
-    back = lax.all_to_all(back, "seq", 0, 0, tiled=True)
     grad_proj = (
-        back.reshape(seq_count, groups, slice_len, 3, width)
-        .transpose(0, 2, 3, 1, 4)
-        .reshape(row_total, qkv_width)
-    )
-    grad_w_qkv = contract_rows(inputs, grad_proj)
-    grad_bias_q = column_sum(grad_proj[:, :model_width])
-    grad_bias_v = column_sum(grad_proj[:, 2 * model_width :])
-    grad_inputs = grad_sum_one + contract_cols(grad_proj, w_qkv_all)
+        jnp.stack(parts).astype(jnp.bfloat16).transpose(2, 0, 1, 3).reshape(length, 3 * width)
+    )
+    token_part = contract_cols(grad_proj, w_qkv_own).astype(jnp.bfloat16)
+    token_part = lax.all_to_all(
+        token_part.reshape(ring, slice_len, model_width), "seq", 0, 0, tiled=True
+    ).reshape(seq_count, groups, slice_len, model_width)
+    grad_inputs = grad_sum_one.reshape(tokens.shape) + jnp.sum(
+        token_part.astype(jnp.float32), axis=1
+    )
+    grad_w_qkv = contract_rows(seq_inputs, grad_proj)
+    grad_qkv_bias = column_sum(grad_proj)
+
+    def own_columns(values):
+        spread = jnp.zeros((model_width,), jnp.float32)
+        return lax.dynamic_update_slice_in_dim(spread, values, own_group * width, 0)
 
     grads = (
-        grad_bias_q,
-        grad_bias_v,
+        own_columns(grad_qkv_bias[:width]),
+        own_columns(grad_qkv_bias[2 * width :]),
         grad_bias_out,
         grad_gain_one,
         grad_shift_one,
@@ -597,18 +622,25 @@
         [grad_w_qkv, jnp.pad(extra, ((0, 0), (0, 128 - count - fold)))], axis=1
     ).astype(jnp.bfloat16)
     last = lax.all_to_all(
-        last.reshape(devices, own_rows, qkv_width + 128), both, 0, 0, tiled=True
-    )
-    last = jnp.sum(last.astype(jnp.float32), axis=0)
-    sums = [last[:, qkv_width + i] for i in range(count)]
+        last.reshape(devices, own_rows, 3 * width + 128), both, 0, 0, tiled=True
+    ).astype(jnp.float32)
+    last = jnp.sum(last.reshape(-1, groups, own_rows, 3 * width + 128), axis=0)
+    own_qkv = (
+        last[:, :, : 3 * width]
+        .reshape(groups, own_rows, 3, width)
+        .transpose(1, 2, 0, 3)
+        .reshape(own_rows, qkv_width)
+    )
+    tail = jnp.sum(last[:, :, 3 * width :], axis=0)
+    sums = [tail[:, i] for i in range(count)]
     own_up = jnp.concatenate(
         [rest_sum[up_start + i * own_rows : up_start + (i + 1) * own_rows] for i in range(fold)],
         axis=1,
     )
     return (
         result.astype(jnp.bfloat16).reshape(seq_count, slice_len, model_width),
-        grad_inputs.reshape(seq_count, slice_len, model_width),
-        last[:, :qkv_width],
+        grad_inputs,
+        own_qkv,
         sums[0],
         sums[1],
         rest_sum[down_rows : down_rows + own_rows],
@@ -616,7 +648,7 @@
         sums[3],
         sums[4],
         own_up,
-        last[:, qkv_width + count : qkv_width + count + fold].reshape(-1),
+        tail[:, count : count + fold].reshape(-1),
         rest_sum[:down_rows],
         sums[5],
         sums[6],

time: 507 us -> 417 us (0.82)
  blocking collectives: 155 us -> 55.4 us
  local copies, waits for them, and re-layouts: 60.8 us -> 74.9 us
  waiting for transfers between devices: 190 us -> 180 us
    all_to_all x2 -> x1, blocking collectives: 155 us -> 55.4 us  [on_device_packed(): lax.all_to_all(first, both, 0, 0, tiled=True)]
    all_to_all x3 -> x4, waiting for transfers between devices: 180 us -> 156 us  [the longest x1 60.4 us: on_device_packed(): lax.all_to_all(jnp.broadcast_to(tokens[:, None], (seq_count, groups, slic...]
    reduce_scatter x1, waiting for transfers between devices: 0.01 us -> 13.4 us  [on_device_packed(): lax.psum_scatter(packed.reshape(-1, model_width), both, scatter_dimension...]
    another operation x8 -> x10, local copies, waits for them, and re-layouts: 2 us -> 9.39 us  [on_device_packed(): jnp.stack(grads, axis=1)]
    all_to_all x3 -> x4, starting transfers between devices: 11.1 us -> 15.6 us  [the longest x1 4.29 us: on_device_packed(): lax.all_to_all(jnp.broadcast_to(tokens[:, None], (seq_count, groups, slic...]
    unnamed x73 -> x71, local copies, waits for them, and re-layouts: 17.4 us -> 17.2 us
  transfers between devices with their start and end apart: 6 -> 7, of which waited for: 4 -> 6; matrix products, arithmetic and copies ran while one was open for 10% -> 16% of each run, Pallas kernels for 5% -> 6%
where the time goes in v2:
time: 417 us; the launch traced here: 410 us
  waiting for transfers between devices  180 us (43%)
  local copies, waits for them, and re-layouts  74.9 us (18%)
  blocking collectives  55.4 us (13%)
  matrix products  31.7 us (8%)
  Pallas kernels  25.6 us (6%)
  starting transfers between devices  19.5 us (5%)
  between operations  15.2 us (4%)
  other arithmetic  8.4 us (2%)
    all_to_all x1, waiting for transfers between devices, on_device_packed(): lax.all_to_all(jnp.broadcast_to(tokens[:, None], (seq_count, groups, slic...  60.4 us
    all_to_all x1, blocking collectives, on_device_packed(): lax.all_to_all(first, both, 0, 0, tiled=True)  55.4 us
    all_to_all x1, waiting for transfers between devices, on_device_packed(): lax.all_to_all(token_part.reshape(ring, slice_len, model_width), 'seq', 0...  47.4 us
    all_to_all x1, waiting for transfers between devices, on_device_packed(): lax.all_to_all(last.reshape(devices, own_rows, 3 * width + 128), both, 0,...  44.8 us
    unnamed x71, local copies, waits for them, and re-layouts  17.2 us
    pallas_call x1, Pallas kernels, local_backward(): pl.pallas_call(backward_kernel, grid=(heads, length // rows), in_specs=[o...  15.6 us
    reduce_scatter x1, waiting for transfers between devices, on_device_packed(): lax.psum_scatter(packed.reshape(-1, model_width), both, scatter_dimension...  13.4 us
    dot_general x4, matrix products, contract_cols(): lax.dot_general(first_op, second_op, (((1,), (1,)), ((), ())), preferred_...  11.4 us
  transfers between devices with their start and end apart: 7, of which 6 were waited for; matrix products, arithmetic and copies ran while one was open for 16% of the time, Pallas kernels for 6%

profile of v2, /device:TPU:0, one launch (start us, length us, event | category | flops | bytes accessed | tf_op | source)
XLA Modules:
  0.0 410.3 jit_solution(235228239758870092)
XLA Ops:
  21.2 55.4 %all_to_all.30 = bf16[32,24,704]{2,1,0:T(8,128)(2,1)S(1)} all-to-all(bf16[32,24,704]{2,1,0:T(8,128)(2,1)S(1)} %bitcast.129), channel_id=1, replica_groups=mesh['dp'=4,'seq'=8] {'dp','seq'}, dimensions={0} | all-to-all | bytes 2162688 | tf_op jit(solution)/shard_map/all_to_all | solution.py:487
  76.6 1.3 broadcast_in_dim.20
  77.9 4.3 %all-to-all-start.1 = ((bf16[8,128,768]{2,1,0:T(8,128)(2,1)}), bf16[8,128,768]{2,1,0:T(8,128)(2,1)}, u32[]{:S(2)}, u32[]{:S(2)}) async-start(bf16[8,128,768]{2,1,0:T(8,128)(2,1)} %bitcast.12), calls=%async_computation.1 | async-start | bytes 3145728 | tf_op jit(solution)/shard_map/all_to_all | solution.py:496
  83.4 2.0 slice_reduce_fusion.1
  85.7 60.4 %all-to-all-done.1 = bf16[8,128,768]{2,1,0:T(8,128)(2,1)} async-done(((bf16[8,128,768]{2,1,0:T(8,128)(2,1)}), bf16[8,128,768]{2,1,0:T(8,128)(2,1)}, u32[]{:S(2)}, u32[]{:S(2)}) %all-to-all-start.1) | async-done | bytes 1572896 | tf_op jit(solution)/shard_map/all_to_all | solution.py:496
  146.1 2.7 add_convert_fusion.1
  148.8 2.4 copy.152
  151.2 1.8 slice_bitcast_fusion
  153.1 9.9 %shard_map.271 = (bf16[3,1024,64]{2,1,0:T(8,128)(2,1)S(1)}, f32[3,1024,1]{2,1,0:T(8,128)S(1)}) custom-call(bf16[3,1024,64]{2,1,0:T(8,128)(2,1)S(1)} %get-tuple-element.69.q_ref, bf16[3,1024,64]{2,1,0:T(8,128)(2,1)S(1)} %get-tuple-element.68.k_ref, bf16[3,1024,64]{2,1,0:T(8,128)(2,1)S(1)} %get-tuple-element.67.v_ref, s32[1024,1]{1,0:T(8,128)S(1)} %copy-done.2, ...), custom_call_target="tpu_custom_call" | custom-call | flops 3221225472 | bytes 1572864 | tf_op jit(solution)/shard_map/pallas_call | solution.py:395
  163.0 1.1 copy-done.4
  167.0 3.6 all-to-all-start.2
  171.8 10.5 %all-to-all-done.2 = bf16[8,128,192]{1,2,0:T(8,128)(2,1)S(1)} async-done(((bf16[8,128,192]{1,2,0:T(8,128)(2,1)}), bf16[8,128,192]{1,2,0:T(8,128)(2,1)S(1)}, u32[]{:S(2)}, u32[]{:S(2)}) %all-to-all-start.2) | async-done | bytes 393248 | tf_op jit(solution)/shard_map/all_to_all | solution.py:521
  182.8 2.8 slice.209
  185.6 3.1 fusion.33
  189.6 7.8 %multiply_convert_fusion = (bf16[256,3072]{1,0:T(8,128)(2,1)S(1)}, f32[256,3072]{1,0:T(8,128)S(1)}, f32[256,3072]{1,0:T(8,128)S(1)}) fusion(f32[3072]{0:T(1024)S(1)} %copy-done.26, bf16[768,768]{1,0:T(8,128)(2,1)S(1)} %bitcast.142, bf16[768,768]{1,0:T(8,128)(2,1)S(1)} %bitcast.144, bf16[768,768]{1,0:T(8,128)(2,1)S(1)} %bitcast.146, ...), kind=kOutput, calls=%fused_computation.9 | convolution fusion | flops 1279721472 | bytes 13389824 | tf_op jit(solution)/shard_map/dot_general | solution.py:543
  197.5 1.5 fusion.38
  200.2 1.3 fusion.31
  201.7 2.8 fusion.28
  204.4 2.2 multiply_reduce_fusion
  206.6 1.6 convolution_convert_fusion
  208.3 1.4 convolution_convert_fusion.1
  211.5 2.5 constant_dynamic-update-slice_fusion.7
  214.0 1.1 constant_dynamic-update-slice_fusion.6
  217.4 1.1 constant_dynamic-update-slice_fusion.3
  219.7 2.5 convolution_convert_fusion.5
  222.3 1.2 copy.157
  224.3 3.9 all-to-all-start.3
  230.0 1.8 reshape.267
  232.7 1.5 stack.96
  235.1 1.5 stack.97
  236.6 3.2 all-to-all-done.3
  241.7 1.5 copy-done.5
  243.2 15.6 %shard_map.272 = (f32[3,1024,64]{2,1,0:T(8,128)S(1)}, f32[3,1024,64]{2,1,0:T(8,128)S(1)}, f32[3,1024,64]{2,1,0:T(8,128)S(1)}) custom-call(bf16[3,1024,64]{2,1,0:T(8,128)(2,1)S(1)} %get-tuple-element.69.q_ref, bf16[3,1024,64]{2,1,0:T(8,128)(2,1)S(1)} %get-tuple-element.68.k_ref, bf16[3,1024,64]{2,1,0:T(8,128)(2,1)S(1)} %get-tuple-element.67.v_ref, ...), custom_call_target="tpu_custom_call" | custom-call | flops 8053063680 | bytes 3932160 | tf_op jit(solution)/shard_map/pallas_call | solution.py:418
  262.3 1.4 constant_dynamic-update-slice_fusion.8
  264.4 1.4 constant_dynamic-update-slice_fusion.9
  265.9 2.3 concatenate.40
  268.1 1.6 pad.10
  270.8 4.2 %fusion.6 = bf16[768,576]{0,1:T(8,128)(2,1)} fusion(bf16[1024,576]{0,1:T(8,128)(2,1)S(1)} %bitcast.150, bf16[1024,768]{1,0:T(8,128)(2,1)} %bitcast.13), kind=kOutput, calls=%fused_computation.29 | convolution fusion | flops 906412032 | bytes 3637248 | tf_op jit(solution)/shard_map/dot_general | solution.py:27
  275.0 1.6 copy.163
  276.7 1.3 pad_maximum_fusion.1
  277.9 3.8 all-to-all-start.5
  281.8 3.9 convolution_convert_fusion.2
  285.7 44.8 %all-to-all-done.5 = bf16[32,24,704]{2,1,0:T(8,128)(2,1)S(1)} async-done(((bf16[32,24,704]{2,1,0:T(8,128)(2,1)}), bf16[32,24,704]{2,1,0:T(8,128)(2,1)S(1)}, u32[]{:S(2)}, u32[]{:S(2)}) %all-to-all-start.5) | async-done | bytes 1081376 | tf_op jit(solution)/shard_map/all_to_all | solution.py:624
  330.5 3.6 all-to-all-start.4
  337.2 47.4 %all-to-all-done.4 = bf16[8,128,768]{2,1,0:T(8,128)(2,1)S(1)} async-done(((bf16[8,128,768]{2,1,0:T(8,128)(2,1)}), bf16[8,128,768]{2,1,0:T(8,128)(2,1)S(1)}, u32[]{:S(2)}, u32[]{:S(2)}) %all-to-all-start.4) | async-done | bytes 1572896 | tf_op jit(solution)/shard_map/all_to_all | solution.py:595
  385.8 13.4 %reduce-scatter.2.cloned.1.call-done = bf16[216,768]{1,0:T(8,128)(2,1)} async-done(((bf16[6912,768]{1,0:T(8,128)(2,1)}), bf16[216,768]{1,0:T(8,128)(2,1)}) %reduce-scatter.2.cloned.1.call-update) | async-done | bytes 331792 | tf_op jit(solution)/shard_map/reduce_scatter | solution.py:578
  399.2 1.5 fusion.35
  401.4 1.6 slice.232
  (151 shorter events, 43.6 us)
Async XLA Ops:
  7.2 75.1 %copy-start = (s32[2,1024]{1,0:T(2,128)S(1)}, s32[2,1024]{1,0:T(2,128)}, u32[]{:S(2)}) copy-start(s32[2,1024]{1,0:T(2,128)} %param.17) | copy-start | bytes 24580
  7.2 69.4 %copy-start.23 = (bf16[2,128,768]{2,1,0:T(8,128)(2,1)S(1)}, bf16[2,128,768]{2,1,0:T(8,128)(2,1)}, u32[]{:S(2)}) copy-start(bf16[2,128,768]{2,1,0:T(8,128)(2,1)} %param.16) | copy-start | bytes 1179652
  7.2 175.6 %all-gather.3.cloned.1.call-start = ((), (), s32[]{:S(2)}) async-start(), calls=%async_computation.8 | async-start | bytes 10948608 | tf_op jit(solution)/shard_map/all_gather | solution.py:467
  12.1 0.7 copy-start.22
  76.6 69.5 %copy-start.10 = (bf16[32,24,704]{2,1,0:T(8,128)(2,1)}, bf16[32,24,704]{2,1,0:T(8,128)(2,1)S(1)}, u32[]{:S(2)}) copy-start(bf16[32,24,704]{2,1,0:T(8,128)(2,1)S(1)} %all_to_all.30) | copy-start | bytes 3244036
  77.9 68.2 %all-to-all-start.1 = ((bf16[8,128,768]{2,1,0:T(8,128)(2,1)}), bf16[8,128,768]{2,1,0:T(8,128)(2,1)}, u32[]{:S(2)}, u32[]{:S(2)}) async-start(bf16[8,128,768]{2,1,0:T(8,128)(2,1)} %bitcast.12), calls=%async_computation.1 | async-start | bytes 3145728 | tf_op jit(solution)/shard_map/all_to_all | solution.py:496
  151.2 1.8 copy-start.2
  163.0 1.1 copy-start.4
  167.0 15.3 %all-to-all-start.2 = ((bf16[8,128,192]{1,2,0:T(8,128)(2,1)}), bf16[8,128,192]{1,2,0:T(8,128)(2,1)S(1)}, u32[]{:S(2)}, u32[]{:S(2)}) async-start(bf16[8,128,192]{1,2,0:T(8,128)(2,1)} %copy.155), calls=%async_computation.2 | async-start | bytes 786432 | tf_op jit(solution)/shard_map/all_to_all | solution.py:521
  170.6 228.6 %reduce-scatter.2.cloned.1.call-start = ((), (), s32[]{:S(2)}) async-start(), calls=%async_computation.7 | async-start | bytes 10948608 | tf_op jit(solution)/shard_map/reduce_scatter | solution.py:578
  182.8 6.0 %copy-start.12 = (bf16[2,4,128,192]{2,0,3,1:T(2,128)(2,1)}, bf16[2,4,128,192]{2,0,3,1:T(2,128)(2,1)S(1)}, u32[]{:S(2)}) copy-start(bf16[2,4,128,192]{2,0,3,1:T(2,128)(2,1)S(1)} %copy.156) | copy-start | bytes 1179652
  185.6 3.2 copy-start.24
  185.6 3.2 copy-start.29
  188.7 8.7 %copy-start.8 = (bf16[32,24,768]{2,1,0:T(8,128)(2,1)}, bf16[32,24,768]{2,1,0:T(8,128)(2,1)S(1)}, u32[]{:S(2)}) copy-start(bf16[32,24,768]{2,1,0:T(8,128)(2,1)S(1)} %get-tuple-element.58) | copy-start | bytes 3538948
  188.7 0.9 copy-start.26
  189.6 7.8 %copy-start.28 = (f32[768]{0:T(1024)S(1)}, f32[768]{0:T(1024)}, u32[]{:S(2)}) copy-start(f32[768]{0:T(1024)} %get-tuple-element.32) | copy-start | bytes 9220
  197.4 1.8 copy-start.9
  197.5 2.7 copy-start.25
  209.7 1.0 copy-start.13
  210.2 9.5 %copy-start.6 = (f32[256,768]{1,0:T(8,128)}, f32[256,768]{1,0:T(8,128)S(1)}, u32[]{:S(2)}) copy-start(f32[256,768]{1,0:T(8,128)S(1)} %get-tuple-element.49) | copy-start | bytes 2359300
  219.7 9.5 %copy-start.27 = (bf16[768]{0:T(1024)(128)(2,1)S(1)}, bf16[768]{0:T(1024)(128)(2,1)}, u32[]{:S(2)}) copy-start(bf16[768]{0:T(1024)(128)(2,1)} %get-tuple-element.27) | copy-start | bytes 4612
  224.3 15.5 %all-to-all-start.3 = ((bf16[8,128,192]{1,2,0:T(8,128)(2,1)}), bf16[8,128,192]{1,2,0:T(8,128)(2,1)S(1)}, u32[]{:S(2)}, u32[]{:S(2)}) async-start(bf16[8,128,192]{1,2,0:T(8,128)(2,1)} %bitcast.35), calls=%async_computation.3 | async-start | bytes 786432 | tf_op jit(solution)/shard_map/all_to_all | solution.py:588
  240.6 1.1 copy-start.3
  241.7 1.5 copy-start.5
  259.2 6.6 %copy-start.16 = (bf16[768,1]{1,0:T(8,128)(2,1)S(1)}, bf16[768,1]{1,0:T(8,128)(2,1)}, u32[]{:S(2)}) copy-start(bf16[768,1]{1,0:T(8,128)(2,1)} %stack.100) | copy-start | bytes 4612
  259.2 6.6 %copy-start.17 = (bf16[768,1]{1,0:T(8,128)(2,1)S(1)}, bf16[768,1]{1,0:T(8,128)(2,1)}, u32[]{:S(2)}) copy-start(bf16[768,1]{1,0:T(8,128)(2,1)} %stack.99) | copy-start | bytes 4612
  259.2 6.6 %copy-start.18 = (bf16[768,4]{1,0:T(8,128)(2,1)S(1)}, bf16[768,4]{1,0:T(8,128)(2,1)}, u32[]{:S(2)}) copy-start(bf16[768,4]{1,0:T(8,128)(2,1)} %reshape.267) | copy-start | bytes 18436
  259.2 6.6 %copy-start.19 = (bf16[768,1]{1,0:T(8,128)(2,1)S(1)}, bf16[768,1]{1,0:T(8,128)(2,1)}, u32[]{:S(2)}) copy-start(bf16[768,1]{1,0:T(8,128)(2,1)} %stack.95) | copy-start | bytes 4612
  259.2 6.6 %copy-start.20 = (bf16[768,1]{1,0:T(8,128)(2,1)S(1)}, bf16[768,1]{1,0:T(8,128)(2,1)}, u32[]{:S(2)}) copy-start(bf16[768,1]{1,0:T(8,128)(2,1)} %stack.96) | copy-start | bytes 4612
  259.2 6.6 %copy-start.21 = (bf16[768,1]{1,0:T(8,128)(2,1)S(1)}, bf16[768,1]{1,0:T(8,128)(2,1)}, u32[]{:S(2)}) copy-start(bf16[768,1]{1,0:T(8,128)(2,1)} %stack.98) | copy-start | bytes 4612
  270.8 4.3 %copy-start.14 = (bf16[1024,3,3,64]{0,3,2,1:T(8,128)(2,1)}, bf16[1024,3,3,64]{0,3,2,1:T(8,128)(2,1)S(1)}, u32[]{:S(2)}) copy-start(bf16[1024,3,3,64]{0,3,2,1:T(8,128)(2,1)S(1)} %copy.162) | copy-start | bytes 3538948
  270.8 5.9 %copy-start.15 = (bf16[768,128]{1,0:T(8,128)(2,1)S(1)}, bf16[768,128]{1,0:T(8,128)(2,1)}, u32[]{:S(2)}) copy-start(bf16[768,128]{1,0:T(8,128)(2,1)} %pad.10) | copy-start | bytes 589828
  275.0 6.8 %copy-start.11 = (bf16[32,24,704]{2,1,0:T(8,128)(2,1)S(1)}, bf16[32,24,704]{2,1,0:T(8,128)(2,1)}, u32[]{:S(2)}) copy-start(bf16[32,24,704]{2,1,0:T(8,128)(2,1)} %copy-done.10) | copy-start | bytes 3244036
  277.9 52.6 %all-to-all-start.5 = ((bf16[32,24,704]{2,1,0:T(8,128)(2,1)}), bf16[32,24,704]{2,1,0:T(8,128)(2,1)S(1)}, u32[]{:S(2)}, u32[]{:S(2)}) async-start(bf16[32,24,704]{2,1,0:T(8,128)(2,1)} %pad_maximum_fusion.1), calls=%async_computation.5 | async-start | bytes 2359296 | tf_op jit(solution)/shard_map/all_to_all | solution.py:624
  330.5 54.1 %all-to-all-start.4 = ((bf16[8,128,768]{2,1,0:T(8,128)(2,1)}), bf16[8,128,768]{2,1,0:T(8,128)(2,1)S(1)}, u32[]{:S(2)}, u32[]{:S(2)}) async-start(bf16[8,128,768]{2,1,0:T(8,128)(2,1)} %bitcast.134), calls=%async_computation.4 | async-start | bytes 3145728 | tf_op jit(solution)/shard_map/all_to_all | solution.py:595
  334.1 50.7 %copy-start.7 = (f32[256,768]{1,0:T(8,128)S(1)}, f32[256,768]{1,0:T(8,128)}, u32[]{:S(2)}) copy-start(f32[256,768]{1,0:T(8,128)} %copy-done.6) | copy-start | bytes 2359300
  336.4 66.7 %copy-start.1 = (s32[2,1024]{1,0:T(2,128)S(1)}, s32[2,1024]{1,0:T(2,128)}, u32[]{:S(2)}) copy-start(s32[2,1024]{1,0:T(2,128)} %param.17) | copy-start | bytes 24580
Sparse Core Ops, SparseCore 0:
  12.9 131.7 all-gather.2
  219.8 179.3 reduce-scatter.1
